TPU v7x, 32 devices: a whole 2x2x4 slice. The times are simulated.
32 devices in a mesh: dp: 16 (over z, y, x), ctx: 2 (over core).
Axes of the slice: x: 2, y: 2, z: 4, core: 2. Of those that a mesh axis runs over, the one named last changes fastest.
Arguments:
- inputs: bfloat16 [2, 16, 1024, 960], P(None, 'dp', 'ctx'), may hold values from -6 to 6
- segment_ids: int32 [2, 16, 1024], P(None, 'dp'), may hold values from 0 to 3, as said below
- positions: int32 [2, 16, 1024], P(None, 'dp'), may hold values from 0 to 767, as said below
- w_query: bfloat16 [960, 960], P('dp', 'ctx'), may hold values from -0.1875 to 0.1875
- w_key: bfloat16 [960, 320], P('dp', 'ctx'), may hold values from -0.1875 to 0.1875
- w_value: bfloat16 [960, 320], P('dp', 'ctx'), may hold values from -0.1875 to 0.1875
- w_out: bfloat16 [960, 960], P('dp', 'ctx'), may hold values from -0.5 to 0.5
- w_gate: bfloat16 [960, 2560], P('dp', 'ctx'), may hold values from -0.1875 to 0.1875
- w_up: bfloat16 [960, 2560], P('dp', 'ctx'), may hold values from -0.1875 to 0.1875
- w_down: bfloat16 [2560, 960], P('dp', 'ctx'), may hold values from -0.125 to 0.125
- gain_attn: bfloat16 [960], P('dp'), may hold values from 0.5 to 1.5
- gain_ffn: bfloat16 [960], P('dp'), may hold values from 0.5 to 1.5
- cotangent: bfloat16 [2, 16, 1024, 960], P(None, 'dp', 'ctx'), may hold values from -6 to 6
Outputs:
- outputs: bfloat16 [2, 16, 1024, 960], P(None, 'dp', 'ctx')
- grad_inputs: float32 [2, 16, 1024, 960], P(None, 'dp', 'ctx')
- grad_w_query: float32 [960, 960], P('dp', 'ctx')
- grad_w_key: float32 [960, 320], P('dp', 'ctx')
- grad_w_value: float32 [960, 320], P('dp', 'ctx')
- grad_w_out: float32 [960, 960], P('dp', 'ctx')
- grad_w_gate: float32 [960, 2560], P('dp', 'ctx')
- grad_w_up: float32 [960, 2560], P('dp', 'ctx')
- grad_w_down: float32 [2560, 960], P('dp', 'ctx')
- grad_gain_attn: float32 [960], P('dp')
- grad_gain_ffn: float32 [960], P('dp')
Inputs may be any that keep to these rules, and one draw needn't show every extreme that they name: `segment_ids`: along each sequence the ids never fall, each of the 4 ids is used, and one document has exactly 768 tokens. `positions`: the number of earlier tokens of the same document in the sequence.
All inputs are finite; a program needn't handle non-finite values.
Results may differ from a plain program's by a relative error of at most 0.02.
Values may be sent and summed in bfloat16 or wider, within the bound.
No kernel may reach another device: no remote copies, remote signals or barrier semaphores. Data moves between devices by JAX's collectives and lax.ppermute only.
A program may use at most 192 MiB of HBM per device.

v0:
```python
import jax
import jax.numpy as jnp
from jax import lax
from jax.sharding import PartitionSpec as P

HEADS = 15
KV_HEADS = 5
HEAD = 64
MICRO = 2
USES = 1
GROUP = 3


EPSILON = 1e-05
MASKED = -1e30


def matmul(left, right):
    return jnp.dot(left, right, preferred_element_type=jnp.float32)


def inner_rows(left, right):
    return lax.dot_general(
        left, right, (((0,), (0,)), ((), ())), preferred_element_type=jnp.float32
    )


def outer_cols(left, right):
    return lax.dot_general(
        left, right, (((1,), (1,)), ((), ())), preferred_element_type=jnp.float32
    )


def rms_scale(hidden):
    return lax.rsqrt(jnp.mean(hidden * hidden, axis=-1, keepdims=True) + EPSILON)


def rotary_tables(own_positions):
    half_width = HEAD // 2
    frequency = 10000.0 ** (-(jnp.arange(half_width, dtype=jnp.float32) * 2.0 / HEAD))
    angles = own_positions.astype(jnp.float32)[:, None] * frequency[None, :]
    return (jnp.cos(angles)[:, None, :], jnp.sin(angles)[:, None, :])


def rotate(values, cos_table, sin_table):
    half_width = values.shape[-1] // 2
    front_half = values[..., :half_width]
    back_half = values[..., half_width:]
    return jnp.concatenate(
        [
            front_half * cos_table - back_half * sin_table,
            back_half * cos_table + front_half * sin_table,
        ],
        axis=-1,
    )


def fetch_weights(w_query, w_key, w_value, w_out, w_gate, w_up, w_down, gain_attn, gain_ffn):
    wide_shards = (
        lax.all_gather(w_query, "ctx", axis=1, tiled=True),
        lax.all_gather(w_key, "ctx", axis=1, tiled=True),
        lax.all_gather(w_value, "ctx", axis=1, tiled=True),
        lax.all_gather(w_out, "ctx", axis=1, tiled=True),
        lax.all_gather(w_gate, "ctx", axis=1, tiled=True),
        lax.all_gather(w_up, "ctx", axis=1, tiled=True),
        lax.all_gather(w_down, "ctx", axis=1, tiled=True),
    )
    return (
        lax.all_gather(wide_shards[0], "dp", axis=0, tiled=True),
        lax.all_gather(wide_shards[1], "dp", axis=0, tiled=True),
        lax.all_gather(wide_shards[2], "dp", axis=0, tiled=True),
        lax.all_gather(wide_shards[3], "dp", axis=0, tiled=True),
        lax.all_gather(wide_shards[4], "dp", axis=0, tiled=True),
        lax.all_gather(wide_shards[5], "dp", axis=0, tiled=True),
        lax.all_gather(wide_shards[6], "dp", axis=0, tiled=True),
        lax.all_gather(gain_attn, "dp", axis=0, tiled=True),
        lax.all_gather(gain_ffn, "dp", axis=0, tiled=True),
    )


def attend_group(operands, allowed):
    query_group, key_group, value_group = operands
    score_scale = HEAD ** (-0.5)
    allowed_f = allowed.astype(jnp.float32)[None]
    scores = (
        jnp.einsum("gtd,sd->gts", query_group, key_group, preferred_element_type=jnp.float32)
        * score_scale
    )
    scores = jnp.where(allowed[None], scores, MASKED)
    row_top = jnp.max(scores, axis=-1, keepdims=True)
    weights = jnp.exp(scores - row_top) * allowed_f
    row_total = jnp.sum(weights, axis=-1, keepdims=True)
    weights_low = (weights / row_total).astype(jnp.bfloat16)
    attended = jnp.einsum(
        "gts,sd->gtd", weights_low, value_group, preferred_element_type=jnp.float32
    )
    return (attended, (row_top + jnp.log(row_total))[..., 0])


def attend_group_back(operands, allowed):
    query_group, key_group, value_group, grad_group, log_total = operands
    score_scale = HEAD ** (-0.5)
    allowed_f = allowed.astype(jnp.float32)[None]
    scores = (
        jnp.einsum("gtd,sd->gts", query_group, key_group, preferred_element_type=jnp.float32)
        * score_scale
    )
    scores = jnp.where(allowed[None], scores, MASKED)
    weights = jnp.exp(scores - log_total[..., None]) * allowed_f
    weights_low = weights.astype(jnp.bfloat16)
    grad_values = jnp.einsum(
        "gts,gtd->sd", weights_low, grad_group, preferred_element_type=jnp.float32
    )
    grad_weights = jnp.einsum(
        "gtd,sd->gts", grad_group, value_group, preferred_element_type=jnp.float32
    )
    grad_scores = (
        weights * (grad_weights - jnp.sum(grad_weights * weights, axis=-1, keepdims=True))
    ).astype(jnp.bfloat16)
    grad_queries = (
        jnp.einsum("gts,sd->gtd", grad_scores, key_group, preferred_element_type=jnp.float32)
        * score_scale
    )
    grad_key_rows = (
        jnp.einsum("gts,gtd->sd", grad_scores, query_group, preferred_element_type=jnp.float32)
        * score_scale
    )
    return (grad_queries, grad_key_rows, grad_values)


def split_groups(queries, key_full, value_full, tok_rows, seq_len):
    query_groups = queries.reshape(tok_rows, KV_HEADS, GROUP, HEAD).transpose(1, 2, 0, 3)
    key_groups = key_full.reshape(seq_len, KV_HEADS, HEAD).transpose(1, 0, 2)
    value_groups = value_full.reshape(seq_len, KV_HEADS, HEAD).transpose(1, 0, 2)
    return (query_groups, key_groups, value_groups)


def collect_key_grads(grad_key_full, grad_value_full):
    return (
        lax.psum_scatter(grad_key_full, "ctx", scatter_dimension=0, tiled=True),
        lax.psum_scatter(grad_value_full, "ctx", scatter_dimension=0, tiled=True),
    )


def layer_forward(hidden, weights, allowed, cos_table, sin_table):
    w_query, w_key, w_value, w_out, w_gate, w_up, w_down, gain_attn, gain_ffn = weights
    tok_rows = hidden.shape[0]
    seq_len = allowed.shape[1]
    normed = (hidden * rms_scale(hidden) * gain_attn.astype(jnp.float32)).astype(jnp.bfloat16)
    queries = (
        rotate(matmul(normed, w_query).reshape(tok_rows, HEADS, HEAD), cos_table, sin_table)
        .astype(jnp.bfloat16)
        .reshape(tok_rows, HEADS * HEAD)
    )
    key_own = (
        rotate(matmul(normed, w_key).reshape(tok_rows, KV_HEADS, HEAD), cos_table, sin_table)
        .astype(jnp.bfloat16)
        .reshape(tok_rows, KV_HEADS * HEAD)
    )
    value_own = matmul(normed, w_value).astype(jnp.bfloat16)
    key_full, value_full = (
        lax.all_gather(key_own, "ctx", axis=0, tiled=True),
        lax.all_gather(value_own, "ctx", axis=0, tiled=True),
    )
    query_groups, key_groups, value_groups = split_groups(
        queries, key_full, value_full, tok_rows, seq_len
    )
    attended, log_total = lax.map(
        lambda operands: attend_group(operands, allowed), (query_groups, key_groups, value_groups)
    )
    attn_low = attended.transpose(2, 0, 1, 3).reshape(tok_rows, HEADS * HEAD).astype(jnp.bfloat16)
    middle = hidden + matmul(attn_low, w_out)
    normed_ffn = (middle * rms_scale(middle) * gain_ffn.astype(jnp.float32)).astype(jnp.bfloat16)
    gate_pre = matmul(normed_ffn, w_gate)
    up_pre = matmul(normed_ffn, w_up)
    activated = (jax.nn.silu(gate_pre) * up_pre).astype(jnp.bfloat16)
    result = middle + matmul(activated, w_down)
    return (
        result,
        (
            hidden,
            queries,
            key_full,
            value_full,
            attn_low,
            log_total,
            middle,
            normed_ffn,
            gate_pre,
            up_pre,
            activated,
        ),
    )


def layer_backward(kept, grad_out, weights, grads, allowed, cos_table, sin_table):
    w_query, w_key, w_value, w_out, w_gate, w_up, w_down, gain_attn, gain_ffn = weights
    (
        hidden,
        queries,
        key_full,
        value_full,
        attn_low,
        log_total,
        middle,
        normed_ffn,
        gate_pre,
        up_pre,
        activated,
    ) = kept
    tok_rows = hidden.shape[0]
    seq_len = allowed.shape[1]
    gain_one = gain_attn.astype(jnp.float32)
    gain_two = gain_ffn.astype(jnp.float32)
    scale_attn = rms_scale(hidden)
    normal_attn = hidden * scale_attn
    normed = (normal_attn * gain_one).astype(jnp.bfloat16)
    scale_ffn = rms_scale(middle)
    normal_ffn = middle * scale_ffn
    sigmoid_gate = jax.nn.sigmoid(gate_pre)
    grad_ffn = grad_out.astype(jnp.bfloat16)
    grad_activated = outer_cols(grad_ffn, w_down)
    grad_gate = (
        grad_activated * up_pre * sigmoid_gate * (1.0 + gate_pre * (1.0 - sigmoid_gate))
    ).astype(jnp.bfloat16)
    grad_up = (grad_activated * jax.nn.silu(gate_pre)).astype(jnp.bfloat16)
    grad_normed_ffn = outer_cols(grad_gate, w_gate) + outer_cols(grad_up, w_up)
    grad_normal_ffn = grad_normed_ffn * gain_two
    grad_middle = grad_out + scale_ffn * (
        grad_normal_ffn
        - normal_ffn * jnp.mean(grad_normal_ffn * normal_ffn, axis=-1, keepdims=True)
    )
    grad_branch = grad_middle.astype(jnp.bfloat16)
    grad_attended = outer_cols(grad_branch, w_out).astype(jnp.bfloat16)
    query_groups, key_groups, value_groups = split_groups(
        queries, key_full, value_full, tok_rows, seq_len
    )
    grad_groups = grad_attended.reshape(tok_rows, KV_HEADS, GROUP, HEAD).transpose(1, 2, 0, 3)
    grad_q_groups, grad_k_groups, grad_v_groups = lax.map(
        lambda operands: attend_group_back(operands, allowed),
        (query_groups, key_groups, value_groups, grad_groups, log_total),
    )
    grad_key_full = grad_k_groups.transpose(1, 0, 2).reshape(seq_len, KV_HEADS * HEAD)
    grad_value_full = grad_v_groups.transpose(1, 0, 2).reshape(seq_len, KV_HEADS * HEAD)
    grad_key_own, grad_value_own = collect_key_grads(grad_key_full, grad_value_full)
    grad_queries = grad_q_groups.transpose(2, 0, 1, 3).reshape(tok_rows, HEADS, HEAD)
    grad_q_low = (
        rotate(grad_queries, cos_table, -sin_table)
        .reshape(tok_rows, HEADS * HEAD)
        .astype(jnp.bfloat16)
    )
    grad_k_low = (
        rotate(grad_key_own.reshape(tok_rows, KV_HEADS, HEAD), cos_table, -sin_table)
        .reshape(tok_rows, KV_HEADS * HEAD)
        .astype(jnp.bfloat16)
    )
    grad_v_low = grad_value_own.astype(jnp.bfloat16)
    grad_normed = (
        outer_cols(grad_q_low, w_query)
        + outer_cols(grad_k_low, w_key)
        + outer_cols(grad_v_low, w_value)
    )
    grad_normal = grad_normed * gain_one
    grad_hidden = grad_middle + scale_attn * (
        grad_normal - normal_attn * jnp.mean(grad_normal * normal_attn, axis=-1, keepdims=True)
    )
    new_grads = (
        grads[0] + inner_rows(normed, grad_q_low),
        grads[1] + inner_rows(normed, grad_k_low),
        grads[2] + inner_rows(normed, grad_v_low),
        grads[3] + inner_rows(attn_low, grad_branch),
        grads[4] + inner_rows(normed_ffn, grad_gate),
        grads[5] + inner_rows(normed_ffn, grad_up),
        grads[6] + inner_rows(activated, grad_ffn),
        grads[7] + jnp.sum(grad_normed * normal_attn, axis=0),
        grads[8] + jnp.sum(grad_normed_ffn * normal_ffn, axis=0),
    )
    return (grad_hidden, new_grads)


def shards(
    inputs,
    segment_ids,
    positions,
    w_query,
    w_key,
    w_value,
    w_out,
    w_gate,
    w_up,
    w_down,
    gain_attn,
    gain_ffn,
    cotangent,
):
    tok_rows = inputs.shape[2]
    seq_len = segment_ids.shape[2]
    dp_count = lax.axis_size("dp")
    ctx_count = lax.axis_size("ctx")
    token_start = lax.axis_index("ctx") * tok_rows
    shard_list = (w_query, w_key, w_value, w_out, w_gate, w_up, w_down)
    grads = tuple(
        (
            jnp.zeros((item.shape[0] * dp_count, item.shape[1] * ctx_count), jnp.float32)
            for item in shard_list
        )
    )
    grads = grads + (
        jnp.zeros((gain_attn.shape[0] * dp_count,), jnp.float32),
        jnp.zeros((gain_ffn.shape[0] * dp_count,), jnp.float32),
    )
    held_weights = None
    result_list = []
    grad_in_list = []
    key_index = jnp.arange(seq_len, dtype=jnp.int32)
    for micro_index in range(MICRO):
        held_weights = fetch_weights(
            w_query, w_key, w_value, w_out, w_gate, w_up, w_down, gain_attn, gain_ffn
        )
        seg_row = segment_ids[micro_index, 0]
        seg_own = lax.dynamic_slice_in_dim(seg_row, token_start, tok_rows)
        pos_own = lax.dynamic_slice_in_dim(positions[micro_index, 0], token_start, tok_rows)
        query_index = token_start + jnp.arange(tok_rows, dtype=jnp.int32)
        allowed = (key_index[None, :] <= query_index[:, None]) & (
            seg_row[None, :] == seg_own[:, None]
        )
        cos_table, sin_table = rotary_tables(pos_own)
        hidden = inputs[micro_index, 0].astype(jnp.float32)
        use_index = 0
        weights = held_weights
        hidden, kept = layer_forward(hidden, weights, allowed, cos_table, sin_table)
        kept_list = [kept]
        result_list.append(hidden.astype(jnp.bfloat16))
        grad_hidden = cotangent[micro_index, 0].astype(jnp.float32)
        for use_index in reversed(range(USES)):
            weights = held_weights
            grad_hidden, grads = layer_backward(
                kept_list[use_index], grad_hidden, weights, grads, allowed, cos_table, sin_table
            )
        grad_in_list.append(grad_hidden)
    row_sums = (
        lax.psum_scatter(
            grads[0].astype(jnp.bfloat16), "dp", scatter_dimension=0, tiled=True
        ).astype(jnp.float32),
        lax.psum_scatter(
            grads[1].astype(jnp.bfloat16), "dp", scatter_dimension=0, tiled=True
        ).astype(jnp.float32),
        lax.psum_scatter(
            grads[2].astype(jnp.bfloat16), "dp", scatter_dimension=0, tiled=True
        ).astype(jnp.float32),
        lax.psum_scatter(
            grads[3].astype(jnp.bfloat16), "dp", scatter_dimension=0, tiled=True
        ).astype(jnp.float32),
        lax.psum_scatter(
            grads[4].astype(jnp.bfloat16), "dp", scatter_dimension=0, tiled=True
        ).astype(jnp.float32),
        lax.psum_scatter(
            grads[5].astype(jnp.bfloat16), "dp", scatter_dimension=0, tiled=True
        ).astype(jnp.float32),
        lax.psum_scatter(
            grads[6].astype(jnp.bfloat16), "dp", scatter_dimension=0, tiled=True
        ).astype(jnp.float32),
        lax.psum_scatter(
            grads[7].astype(jnp.bfloat16), "dp", scatter_dimension=0, tiled=True
        ).astype(jnp.float32),
        lax.psum_scatter(
            grads[8].astype(jnp.bfloat16), "dp", scatter_dimension=0, tiled=True
        ).astype(jnp.float32),
    )
    tiled_attn = jnp.broadcast_to(row_sums[7][None, :], (ctx_count, row_sums[7].shape[0]))
    tiled_ffn = jnp.broadcast_to(row_sums[8][None, :], (ctx_count, row_sums[8].shape[0]))
    col_sums = (
        lax.psum_scatter(
            row_sums[0].astype(jnp.bfloat16), "ctx", scatter_dimension=1, tiled=True
        ).astype(jnp.float32),
        lax.psum_scatter(
            row_sums[1].astype(jnp.bfloat16), "ctx", scatter_dimension=1, tiled=True
        ).astype(jnp.float32),
        lax.psum_scatter(
            row_sums[2].astype(jnp.bfloat16), "ctx", scatter_dimension=1, tiled=True
        ).astype(jnp.float32),
        lax.psum_scatter(
            row_sums[3].astype(jnp.bfloat16), "ctx", scatter_dimension=1, tiled=True
        ).astype(jnp.float32),
        lax.psum_scatter(
            row_sums[4].astype(jnp.bfloat16), "ctx", scatter_dimension=1, tiled=True
        ).astype(jnp.float32),
        lax.psum_scatter(
            row_sums[5].astype(jnp.bfloat16), "ctx", scatter_dimension=1, tiled=True
        ).astype(jnp.float32),
        lax.psum_scatter(
            row_sums[6].astype(jnp.bfloat16), "ctx", scatter_dimension=1, tiled=True
        ).astype(jnp.float32),
        lax.psum_scatter(
            tiled_attn.astype(jnp.bfloat16), "ctx", scatter_dimension=0, tiled=True
        ).astype(jnp.float32),
        lax.psum_scatter(
            tiled_ffn.astype(jnp.bfloat16), "ctx", scatter_dimension=0, tiled=True
        ).astype(jnp.float32),
    )
    outputs = jnp.stack(result_list)[:, None]
    grad_inputs = jnp.stack(grad_in_list)[:, None]
    return (
        outputs,
        grad_inputs,
        col_sums[0],
        col_sums[1],
        col_sums[2],
        col_sums[3],
        col_sums[4],
        col_sums[5],
        col_sums[6],
        col_sums[7][0],
        col_sums[8][0],
    )


def solution(mesh):
    return jax.shard_map(
        shards,
        mesh=mesh,
        in_specs=(
            P(None, "dp", "ctx", None),
            P(None, "dp", None),
            P(None, "dp", None),
            P("dp", "ctx"),
            P("dp", "ctx"),
            P("dp", "ctx"),
            P("dp", "ctx"),
            P("dp", "ctx"),
            P("dp", "ctx"),
            P("dp", "ctx"),
            P("dp"),
            P("dp"),
            P(None, "dp", "ctx", None),
        ),
        out_specs=(
            P(None, "dp", "ctx", None),
            P(None, "dp", "ctx", None),
            P("dp", "ctx"),
            P("dp", "ctx"),
            P("dp", "ctx"),
            P("dp", "ctx"),
            P("dp", "ctx"),
            P("dp", "ctx"),
            P("dp", "ctx"),
            P("dp"),
            P("dp"),
        ),
        check_vma=False,
    )
```

profile of v0, /device:TPU:0, one launch (start us, length us, event | category | flops | bytes accessed | tf_op | source)
XLA Modules:
  0.0 1225.3 jit_solution(13575665580968405000)
XLA Ops:
  26.2 43.4 %all-reduce.19 = (bf16[960]{0:T(1024)(128)(2,1)S(1)}, bf16[960]{0:T(1024)(128)(2,1)S(1)}) all-reduce(bf16[960]{0:T(1024)(128)(2,1)S(1)} %dynamic-update-slice, bf16[960]{0:T(1024)(128)(2,1)S(1)} %dynamic-update-slice.1), channel_id=1, replica_groups=mesh['dp'=16,'ctx'=2] {'dp'}, use_global_device_ids=true, to_apply=%add | all-reduce | flops 1920 | bytes 7680
  71.7 41.1 %all-gather.3 = bf16[16,60,320]{2,1,0:T(8,128)(2,1)S(1)} all-gather(bf16[1,60,320]{2,1,0:T(8,128)(2,1)S(1)} %bitcast.599), channel_id=1, replica_groups=mesh['dp'=16,'ctx'=2] {'dp'}, dimensions={0}, use_global_device_ids=true | all-gather | bytes 652800 | tf_op jit(solution)/shard_map/all_gather | solution.py:70
  116.5 46.1 %all-gather.5 = bf16[16,60,320]{2,1,0:T(8,128)(2,1)} all-gather(bf16[1,60,320]{2,1,0:T(8,128)(2,1)S(1)} %bitcast.600), channel_id=1, replica_groups=mesh['dp'=16,'ctx'=2] {'dp'}, dimensions={0}, use_global_device_ids=true | all-gather | bytes 652800 | tf_op jit(solution)/shard_map/all_gather | solution.py:71
  200.9 41.0 %while.56 = (s32[]{:T(128)}, bf16[5,3,512,64]{2,3,1,0:T(8,128)(2,1)S(1)}, f32[5,3,512]{2,1,0:T(4,128)S(1)}, bf16[5,3,512,64]{2,3,1,0:T(8,128)(2,1)}, bf16[5,1024...) while((s32[]{:T(128)}, ...), condition=%wide.region_4.5_spmd.clone, body=%wide.region_1.4_spmd.clone.sunk | while | flops 426768896 | bytes 28184688 | solution.py:168
  252.0 41.2 %while.57 = (s32[]{:T(128)}, bf16[5,3,512,64]{2,3,1,0:T(8,128)(2,1)S(1)}, f32[5,3,512]{2,1,0:T(4,128)S(1)}, bf16[5,3,512,64]{2,3,1,0:T(8,128)(2,1)}, bf16[5,1024...) while((s32[]{:T(128)}, ...), condition=%wide.region_10.11_spmd.clone, body=%wide.region_7.10_spmd.clone.sunk | while | flops 426768896 | bytes 28184688 | solution.py:168
  298.0 7.7 reshape.574
  305.6 12.6 %all-gather.25.cloned.1.call-done = bf16[16,60,2560]{2,1,0:T(8,128)(2,1)} async-done(((bf16[1,60,2560]{2,1,0:T(8,128)(2,1)}), bf16[16,60,2560]{2,1,0:T(8,128)(2,1)}) %all-gather.25.cloned.1.call-update) | async-done | bytes 4915216 | tf_op jit(solution)/shard_map/all_gather | solution.py:74
  318.3 7.4 reshape.576
  325.6 7.2 fusion.216
  337.5 67.7 %all-gather.17.cloned.1.call-done = bf16[2560,960]{1,0:T(8,128)(2,1)} async-done(((bf16[160,960]{1,0:T(8,128)(2,1)}), bf16[2560,960]{1,0:T(8,128)(2,1)}) %all-gather.17.cloned.1.call-update) | async-done | bytes 4915216 | tf_op jit(solution)/shard_map/all_gather | solution.py:75
  405.2 10.4 multiply_convert_fusion.4
  415.7 6.8 fusion.220
  422.5 7.5 multiply_reduce_fusion.3
  436.0 9.6 multiply_convert_fusion.2
  460.8 69.1 %while.59 = (s32[]{:T(128)}, f32[5,3,512,64]{2,3,1,0:T(8,128)}, f32[5,1024,64]{1,2,0:T(8,128)}, f32[5,1024,64]{1,2,0:T(8,128)}, bf16[5,3,512,64]{2,3,1,0:T(8,128...) while((s32[]{:T(128)}, f32[5,3,512,64]{2,3,1,0:T(8,128)}, ...), condition=%wide.region_22.23_spmd.clone, body=%wide.region_20.22_spmd.clone.sunk | while | flops 1024621056 | bytes 62434496 | solution.py:239
  535.5 68.8 %while.58 = (s32[]{:T(128)}, f32[5,3,512,64]{2,3,1,0:T(8,128)S(1)}, f32[5,1024,64]{1,2,0:T(8,128)}, f32[5,1024,64]{1,2,0:T(8,128)}, bf16[5,3,512,64]{2,3,1,0:T(8...) while((s32[]{:T(128)}, f32[5,3,512,64]{2,3,1,0:T(8,128)S(1)}, ...), condition=%wide.region_15.16_spmd.clone, body=%wide.region_13.15_spmd.clone.sunk | while | flops 1024621056 | bytes 62434496 | solution.py:239
  617.0 4.9 add_convert_fusion
  623.6 6.2 fusion.157
  629.8 5.3 fusion.156
  653.9 6.3 add_convert_fusion.2
  676.6 412.9 %fusion.211 = (bf16[64,960]{1,0:T(8,128)(2,1)}, bf16[64,320]{1,0:T(8,128)(2,1)}, bf16[64,320]{1,0:T(8,128)(2,1)S(1)}, bf16[64,960]{1,0:T(8,128)(2,1)S(1)}, bf16[...) fusion(bf16[960,960]{1,0:T(8,128)(2,1)} %add_convert_fusion.4, bf16[960,320]{1,0:T(8,128)(2,1)} %add_convert_fusion.8, ...), kind=kCustom, calls=%all-reduce-scatter.6 | all-reduce-scatter fusion | flops 7864321 | bytes 15729152
  1138.9 5.4 concatenate.54
  1146.4 5.4 fusion.142
  1151.8 38.3 %all-reduce.18 = (bf16[960]{0:T(1024)(128)(2,1)S(1)}, bf16[960]{0:T(1024)(128)(2,1)S(1)}) all-reduce(bf16[960]{0:T(1024)(128)(2,1)S(1)} %add_convert_fusion.14, bf16[960]{0:T(1024)(128)(2,1)S(1)} %copy-done.78), channel_id=20, replica_groups=mesh['dp'=16,'ctx'=2] {'dp'}, use_global_device_ids=true, to_apply=%region_42.43.clone | all-reduce | flops 1920 | bytes 7680
  (584 shorter events, 454.6 us)
Async XLA Ops:
  7.2 179.1 %all-gather.19.cloned.1.call-start = ((), (), s32[]{:S(2)}) async-start(), calls=%async_computation.20 | async-start | bytes 2228224 | tf_op jit(solution)/shard_map/all_gather | solution.py:69
  10.5 231.4 %all-gather.21.cloned.1.call-start = ((), (), s32[]{:S(2)}) async-start(), calls=%async_computation.21 | async-start | bytes 2228224 | tf_op jit(solution)/shard_map/all_gather | solution.py:72
  13.6 284.3 %all-gather.23.cloned.1.call-start = ((), (), s32[]{:S(2)}) async-start(), calls=%async_computation.22 | async-start | bytes 5570560 | tf_op jit(solution)/shard_map/all_gather | solution.py:73
  17.6 300.7 %all-gather.25.cloned.1.call-start = ((), (), s32[]{:S(2)}) async-start(), calls=%async_computation.23 | async-start | bytes 5570560 | tf_op jit(solution)/shard_map/all_gather | solution.py:74
  19.9 385.3 %all-gather.17.cloned.1.call-start = ((), (), s32[]{:S(2)}) async-start(), calls=%async_computation.12 | async-start | bytes 5570560 | tf_op jit(solution)/shard_map/all_gather | solution.py:75
  23.4 641.2 %reduce-scatter.39.cloned.1.call-start = ((), (), s32[]{:S(2)}) async-start(), calls=%async_computation.15 | async-start | bytes 1966080 | tf_op jit(solution)/shard_map/reduce_scatter | solution.py:140
  529.9 136.6 %reduce-scatter.35.cloned.1.call-start = ((), (), s32[]{:S(2)}) async-start(), calls=%async_computation.13 | async-start | bytes 1966080 | tf_op jit(solution)/shard_map/reduce_scatter | solution.py:140
  604.3 66.0 %reduce-scatter.37.cloned.1.call-start = ((), (), s32[]{:S(2)}) async-start(), calls=%async_computation.14 | async-start | bytes 1966080 | tf_op jit(solution)/shard_map/reduce_scatter | solution.py:141
  605.0 68.9 %reduce-scatter.41.cloned.1.call-start = ((), (), s32[]{:S(2)}) async-start(), calls=%async_computation.16 | async-start | bytes 1966080 | tf_op jit(solution)/shard_map/reduce_scatter | solution.py:141
  607.0 591.3 %reduce-scatter.47.cloned.1.call-start = ((), (), s32[]{:S(2)}) async-start(), calls=%async_computation.19 | async-start | bytes 5570560 | tf_op jit(solution)/shard_map/reduce_scatter | solution.py:360
  621.9 585.0 %reduce-scatter.51.cloned.1.call-start = ((), (), s32[]{:S(2)}) async-start(), calls=%async_computation.25 | async-start | bytes 122880
  676.6 415.0 %copy-start.8 = (bf16[960,320]{1,0:T(8,128)(2,1)S(1)}, bf16[960,320]{1,0:T(8,128)(2,1)}, u32[]{:S(2)}) copy-start(bf16[960,320]{1,0:T(8,128)(2,1)} %copy-done.7) | copy-start | bytes 1843204
  1090.4 17.6 %collective-permute-start.1 = (bf16[60,320]{1,0:T(8,128)(2,1)S(1)}, bf16[60,320]{1,0:T(8,128)(2,1)S(1)}, u32[]{:S(2)}, u32[]{:S(2)}) collective-permute-start(bf16[60,320]{1,0:T(8,128)(2,1)S(1)} %slice.113), channel_id=1, source_target_pairs={{0,2},{2,4},{4,6},{6,8},{8,10},{10,12},{12,14},{14,16},{16,18},{18... | collective-permute-start | bytes 115208
  1097.2 25.8 %collective-permute-start = (bf16[60,960]{1,0:T(8,128)(2,1)}, bf16[60,960]{1,0:T(8,128)(2,1)}, u32[]{:S(2)}, u32[]{:S(2)}) collective-permute-start(bf16[60,960]{1,0:T(8,128)(2,1)} %slice.112), channel_id=1, source_target_pairs={{0,2},{2,4},{4,6},{6,8},{8,10},{10,12},{12,14},{14,16},{16,18},{18... | collective-permute-start | bytes 345608
  1099.8 18.7 %collective-permute-start.2 = (bf16[60,320]{1,0:T(8,128)(2,1)}, bf16[60,320]{1,0:T(8,128)(2,1)}, u32[]{:S(2)}, u32[]{:S(2)}) collective-permute-start(bf16[60,320]{1,0:T(8,128)(2,1)} %slice.114), channel_id=1, source_target_pairs={{0,2},{2,4},{4,6},{6,8},{8,10},{10,12},{12,14},{14,16},{16,18},{18... | collective-permute-start | bytes 115208
  1102.4 31.6 %collective-permute-start.3 = (bf16[60,960]{1,0:T(8,128)(2,1)}, bf16[60,960]{1,0:T(8,128)(2,1)}, u32[]{:S(2)}, u32[]{:S(2)}) collective-permute-start(bf16[60,960]{1,0:T(8,128)(2,1)} %slice.115), channel_id=1, source_target_pairs={{0,2},{2,4},{4,6},{6,8},{8,10},{10,12},{12,14},{14,16},{16,18},{18... | collective-permute-start | bytes 345608
  1105.1 33.8 %collective-permute-start.4 = (bf16[60,2560]{1,0:T(8,128)(2,1)}, bf16[60,2560]{1,0:T(8,128)(2,1)}, u32[]{:S(2)}, u32[]{:S(2)}) collective-permute-start(bf16[60,2560]{1,0:T(8,128)(2,1)} %slice.116), channel_id=1, source_target_pairs={{0,2},{2,4},{4,6},{6,8},{8,10},{10,12},{12,14},{14,16},{16,18},{18... | collective-permute-start | bytes 921608
  1108.6 84.2 %collective-permute-start.5 = (bf16[60,2560]{1,0:T(8,128)(2,1)}, bf16[60,2560]{1,0:T(8,128)(2,1)}, u32[]{:S(2)}, u32[]{:S(2)}) collective-permute-start(bf16[60,2560]{1,0:T(8,128)(2,1)} %slice.117), channel_id=1, source_target_pairs={{0,2},{2,4},{4,6},{6,8},{8,10},{10,12},{12,14},{14,16},{16,18},{18... | collective-permute-start | bytes 921608
  1118.5 90.0 %reduce-scatter.53.cloned.1.call-start = ((), (), s32[]{:S(2)}) async-start(), calls=%async_computation.26 | async-start | bytes 122880
  1123.0 87.0 %reduce-scatter.49.cloned.1.call-start = ((), (), s32[]{:S(2)}) async-start(), calls=%async_computation.24 | async-start | bytes 368640
  1129.6 82.1 %reduce-scatter.55.cloned.1.call-start = ((), (), s32[]{:S(2)}) async-start(), calls=%async_computation.27 | async-start | bytes 368640
  1138.8 74.5 %reduce-scatter.43.cloned.1.call-start = ((), (), s32[]{:S(2)}) async-start(), calls=%async_computation.17 | async-start | bytes 491520 | tf_op jit(solution)/shard_map/reduce_scatter | solution.py:385
  1146.2 68.9 %reduce-scatter.45.cloned.1.call-start = ((), (), s32[]{:S(2)}) async-start(), calls=%async_computation.18 | async-start | bytes 491520 | tf_op jit(solution)/shard_map/reduce_scatter | solution.py:388
  1196.0 20.7 %reduce-scatter.57.cloned.1.call-start = ((), (), s32[]{:S(2)}) async-start(), calls=%async_computation.28 | async-start | bytes 737280
  (116 other events, 1083.1 us)
Sparse Core Ops, SparseCore 0:
  11.4 66.5 all-gather.18
  81.3 63.6 all-gather.20
  147.8 84.0 all-gather.22
  234.5 83.7 all-gather.24
  321.5 83.7 all-gather.16
  530.0 7.3 reduce-scatter.38
  604.4 7.3 reduce-scatter.34
  614.0 9.9 reduce-scatter.36
  626.4 9.9 reduce-scatter.40
  638.5 206.2 reduce-scatter.46
  1118.6 10.9 reduce-scatter.50
  1131.7 8.6 reduce-scatter.52
  1142.6 8.7 reduce-scatter.48
  1154.0 8.7 reduce-scatter.54
  1165.5 8.8 reduce-scatter.42
  1196.2 3.7 reduce-scatter.44
  1202.1 9.0 reduce-scatter.56
where the time goes:
time: 1240 us; the launch traced here: 1230 us
  blocking collectives  613 us (49%)
  matrix products  334 us (27%)
  local copies, waits for them, and re-layouts  96.7 us (8%)
  waiting for transfers between devices  81.4 us (7%)
  other arithmetic  67.7 us (5%)
  between operations  17.4 us (1%)
  starting transfers between devices  14.2 us (1%)
    unnamed x4, blocking collectives  497 us
    unnamed x241, local copies, waits for them, and re-layouts  80.5 us
    all_gather x1, waiting for transfers between devices, fetch_weights(): lax.all_gather(wide_shards[6], 'dp', axis=0, tiled=True)  67.7 us
    dot_general x14, matrix products, outer_cols(): lax.dot_general(left, right, (((1,), (1,)), ((), ())), preferred_element_...  66 us
    dot_general x14, matrix products, matmul(): return jnp.dot(left, right, preferred_element_type=jnp.float32)  49 us
    all_gather x1, blocking collectives, fetch_weights(): lax.all_gather(wide_shards[2], 'dp', axis=0, tiled=True)  46.1 us
    all_gather x1, blocking collectives, fetch_weights(): lax.all_gather(wide_shards[1], 'dp', axis=0, tiled=True)  41.1 us
    dot_general x14, matrix products, inner_rows(): lax.dot_general(left, right, (((0,), (0,)), ((), ())), preferred_element_...  40.1 us
  transfers between devices with their start and end apart: 23, of which 2 were waited for; matrix products, arithmetic and copies ran while one was open for 63% of the time, Pallas kernels for 0%

commit v1 on v0

v1 whole, which is shorter than its diff:
```python
import functools

import jax
import jax.numpy as jnp
from jax import lax
from jax.experimental import pallas as pl
from jax.experimental.pallas import tpu as pltpu
from jax.sharding import PartitionSpec as P

HEADS = 15
KV_HEADS = 5
HEAD = 64
MICRO = 2
GROUP = 3
DOCS = 4

EPSILON = 1e-05
MASKED = -1e30
LANES = 128
QKV = (HEADS + 2 * KV_HEADS) * HEAD
QKV_PAD = 1664
VMEM_LIMIT = 60 * 1024 * 1024
F32 = jnp.float32
BF16 = jnp.bfloat16


def up(value, step):
    return -(-value // step) * step


def mm(left, right):
    return lax.dot_general(left, right, (((1,), (0,)), ((), ())), preferred_element_type=F32)


def mm_nt(left, right):
    return lax.dot_general(left, right, (((1,), (1,)), ((), ())), preferred_element_type=F32)


def mm_tn(left, right):
    return lax.dot_general(left, right, (((0,), (0,)), ((), ())), preferred_element_type=F32)


def call(body, out_shape, grid, in_specs, out_specs, scratch=(), flops=0, moved=0, prefetch=0, alias=None):
    return pl.pallas_call(
        body,
        out_shape=out_shape,
        grid_spec=pltpu.PrefetchScalarGridSpec(
            num_scalar_prefetch=prefetch,
            grid=grid,
            in_specs=in_specs,
            out_specs=out_specs,
            scratch_shapes=scratch,
        ),
        input_output_aliases=alias or {},
        compiler_params=pltpu.CompilerParams(vmem_limit_bytes=VMEM_LIMIT),
        cost_estimate=pl.CostEstimate(flops=flops, bytes_accessed=moved, transcendentals=0),
    )


def whole(shape):
    return pl.BlockSpec(shape, lambda *_: (0,) * len(shape))


def lane_of(rows):
    return lax.broadcasted_iota(jnp.int32, (rows, LANES), 1)


def three_terms(column):
    high = column.astype(BF16).astype(F32)
    rest = column - high
    mid = rest.astype(BF16).astype(F32)
    return high, mid, rest - mid


def put_terms(base, column, lane, first):
    high, mid, low = three_terms(column)
    base = jnp.where(lane == first, high, base)
    base = jnp.where(lane == first + 1, mid, base)
    return jnp.where(lane == first + 2, low, base)


def pre_body(width, x_ref, e_ref, w_ref, gain_ref, cos_ref, sa_ref, sb_ref, aq_ref, ak_ref,
             xp_ref, a_ref, q_ref, k_ref, v_ref):
    xp = mm(x_ref[...], e_ref[:width, :])
    scale = lax.rsqrt(jnp.sum(xp * xp, axis=-1, keepdims=True) / width + EPSILON)
    a = (xp * scale * gain_ref[...]).astype(BF16)
    xp_ref[...] = xp.astype(BF16)
    a_ref[...] = a
    t = mm(a, w_ref[...])
    lane = lane_of(t.shape[0])
    low = lane < HEAD
    cos, sa, sb, aq, ak = cos_ref[...], sa_ref[...], sb_ref[...], aq_ref[...], ak_ref[...]
    for pair in range((HEADS + KV_HEADS) // 2):
        tt = t[:, LANES * pair : LANES * (pair + 1)]
        rot = tt * cos + pltpu.roll(tt, 32, 1) * sa + pltpu.roll(tt, 96, 1) * sb
        for half in range(2):
            head = 2 * pair + half
            val = rot if half == 0 else pltpu.roll(rot, 64, 1)
            if head < HEADS:
                q_ref[head] = jnp.where(low, val * HEAD ** -0.5, aq).astype(BF16)
            else:
                k_ref[head - HEADS] = jnp.where(low, val, ak).astype(BF16)
    av = jnp.where(lane < HEAD + 3, -1.0, 0.0)
    for head in range(KV_HEADS):
        first = (HEADS + KV_HEADS) * HEAD + LANES * (head // 2)
        tt = t[:, first : first + LANES]
        val = tt if head % 2 == 0 else pltpu.roll(tt, 64, 1)
        v_ref[head] = jnp.where(low, val, av).astype(BF16)


def pre_attention(x, spread, w_qkv, gain, cos, sa, sb, aq, ak, block=256):
    seq, width = x.shape
    wide = spread.shape[1]
    rows = lambda n: pl.BlockSpec((block, n), lambda i: (i, 0))
    heads = lambda n: pl.BlockSpec((n, block, LANES), lambda i: (0, i, 0))
    return call(
        functools.partial(pre_body, width),
        [
            jax.ShapeDtypeStruct((seq, wide), BF16),
            jax.ShapeDtypeStruct((seq, wide), BF16),
            jax.ShapeDtypeStruct((HEADS, seq, LANES), BF16),
            jax.ShapeDtypeStruct((KV_HEADS, seq, LANES), BF16),
            jax.ShapeDtypeStruct((KV_HEADS, seq, LANES), BF16),
        ],
        (seq // block,),
        [rows(width), whole(spread.shape), whole(w_qkv.shape), whole((1, wide))]
        + [rows(LANES)] * 5,
        [rows(wide), rows(wide), heads(HEADS), heads(KV_HEADS), heads(KV_HEADS)],
        flops=2 * seq * wide * (width + QKV_PAD),
        moved=20_000_000,
    )(x, spread, w_qkv, gain, cos, sa, sb, aq, ak)


def attend_body(block, q_ref, k_ref, v_ref, o_ref, q2_ref):
    seq = k_ref.shape[1]
    rows = GROUP * block
    below = lax.broadcasted_iota(jnp.int32, (block, block), 0) >= lax.broadcasted_iota(
        jnp.int32, (block, block), 1
    )
    below = jnp.concatenate([below.astype(F32)] * GROUP, axis=0) > 0.5
    lane = lane_of(rows)
    for i in range(seq // block):
        span = slice(block * i, block * (i + 1))
        q = q_ref[:, span, :].reshape(rows, LANES)
        s_in = jnp.where(below, mm_nt(q, k_ref[0, span, :]), MASKED)
        top = jnp.max(s_in, axis=-1, keepdims=True)
        if i:
            s_left = mm_nt(q, k_ref[0, : block * i, :])
            top = jnp.maximum(top, jnp.max(s_left, axis=-1, keepdims=True))
        ext = mm(jnp.exp(s_in - top).astype(BF16), v_ref[0, span, :])
        if i:
            ext = ext + mm(jnp.exp(s_left - top).astype(BF16), v_ref[0, : block * i, :])
        total = -ext[:, HEAD : HEAD + 1]
        o = ext / total
        o = jnp.where(lane < HEAD, o, pltpu.roll(o, 64, 1))
        o_ref[:, span, :] = o.reshape(GROUP, block, LANES).astype(BF16)
        q2 = put_terms(q.astype(F32), top + jnp.log(total), lane, HEAD + DOCS)
        q2_ref[:, span, :] = q2.reshape(GROUP, block, LANES).astype(BF16)


def attend(q, k, v, block=256):
    seq = q.shape[1]
    group = pl.BlockSpec((GROUP, seq, LANES), lambda n: (n, 0, 0))
    one = pl.BlockSpec((1, seq, LANES), lambda n: (n, 0, 0))
    shape = jax.ShapeDtypeStruct(q.shape, BF16)
    return call(
        functools.partial(attend_body, block),
        [shape, shape],
        (KV_HEADS,),
        [group, one, one],
        [group, group],
        flops=4 * HEADS * seq * seq * LANES,
        moved=15_000_000,
    )(q, k, v)


def attend_back_body(block, q_ref, k_ref, v_ref, do_ref, cos_ref, sa_ref, sb_ref,
                     dq_ref, dk_ref, dv_ref, acc_ref):
    seq = k_ref.shape[1]
    above = lax.broadcasted_iota(jnp.int32, (block, block), 0) <= lax.broadcasted_iota(
        jnp.int32, (block, block), 1
    )
    lane = lane_of(seq)

    def unrotate(t, span):
        rows = span.stop - span.start
        rot = (
            t * cos_ref[span, :]
            - pltpu.roll(t, 32, 1) * sa_ref[span, :]
            - pltpu.roll(t, 96, 1) * sb_ref[span, :]
        )
        return twice(rot, rows)

    def twice(t, rows):
        return jnp.where(lane[:rows] < HEAD, t, pltpu.roll(t, 64, 1)).astype(BF16)

    for j in range(seq // block):
        span = slice(block * j, block * (j + 1))
        k, v = k_ref[0, span, :], v_ref[0, span, :]
        dk = jnp.zeros((block, LANES), F32)
        dv = jnp.zeros((block, LANES), F32)
        for g in range(GROUP):
            q, do = q_ref[g, block * j :, :], do_ref[g, block * j :, :]
            p = jnp.exp(mm_nt(k, q))
            inner = jnp.where(above, p[:, :block], 0.0)
            p = inner if p.shape[1] == block else jnp.concatenate([inner, p[:, block:]], axis=1)
            ds = (p * mm_nt(v, do)).astype(BF16)
            dv = dv + mm(p.astype(BF16), do)
            dk = dk + mm(ds, q)
            dq = mm_tn(ds, k)
            if j == 0:
                acc_ref[g] = dq
            else:
                acc_ref[g, block * j :, :] += dq
        dk_ref[0, span, :] = unrotate(dk, span)
        dv_ref[0, span, :] = twice(dv, block)
    for g in range(GROUP):
        dq_ref[g] = unrotate(acc_ref[g] * HEAD ** -0.5, slice(0, seq))


def attend_back(q, k, v, do, cos, sa, sb, block=256):
    seq = q.shape[1]
    group = pl.BlockSpec((GROUP, seq, LANES), lambda n: (n, 0, 0))
    one = pl.BlockSpec((1, seq, LANES), lambda n: (n, 0, 0))
    return call(
        functools.partial(attend_back_body, block),
        [
            jax.ShapeDtypeStruct(q.shape, BF16),
            jax.ShapeDtypeStruct(k.shape, BF16),
            jax.ShapeDtypeStruct(k.shape, BF16),
        ],
        (KV_HEADS,),
        [group, one, one, group] + [whole((seq, LANES))] * 3,
        [group, one, one],
        scratch=[pltpu.VMEM((GROUP, seq, LANES), F32)],
        flops=10 * HEADS * seq * seq * LANES,
        moved=20_000_000,
    )(q, k, v, do, cos, sa, sb)


def columns_of(w_refs, part):
    w = w_refs[part % 2][:, part // 2]
    return w.reshape(w.shape[0] * w.shape[1], w.shape[2])


def pairs_to(ref, get, heads, first=0):
    for pair in range((heads + 1) // 2):
        left = get(2 * pair)
        lane = lane_of(left.shape[0])
        right = get(2 * pair + 1).astype(F32) if 2 * pair + 1 < heads else 0.0
        both = jnp.where(lane < HEAD, left.astype(F32), right)
        ref[:, first + LANES * pair : first + LANES * (pair + 1)] = both.astype(BF16)


def mid_body(width, o_ref, ct_ref, e_ref, wo0_ref, wo1_ref, xp_ref, gain_ref,
             op_ref, m_ref, b_ref, df_ref, nat_ref):
    pairs_to(nat_ref, lambda h: o_ref[h], HEADS)
    op = mm(nat_ref[...], e_ref[...]).astype(BF16)
    op_ref[...] = op
    square = 0.0
    for part in range(4):
        w = columns_of((wo0_ref, wo1_ref), part)
        cols = slice(w.shape[1] * part, w.shape[1] * (part + 1))
        m = xp_ref[:, cols].astype(F32) + mm(op, w)
        m_ref[:, cols] = m
        square = square + jnp.sum(m * m, axis=-1, keepdims=True)
    b_ref[...] = (m_ref[...] * lax.rsqrt(square / width + EPSILON) * gain_ref[...]).astype(BF16)
    df_ref[...] = mm(ct_ref[...], e_ref[:width, :]).astype(BF16)


def out_spec_of(packed, which):
    return pl.BlockSpec((packed.shape[0], 2, 64, 256), lambda *_: (0, 0, 15 + which, 0))


def middle(o, ct, spread, packed, xp, gain, block=256):
    seq, width = ct.shape
    wide = spread.shape[1]
    rows = lambda n: pl.BlockSpec((block, n), lambda i: (i, 0))
    return call(
        functools.partial(mid_body, width),
        [
            jax.ShapeDtypeStruct((seq, wide), BF16),
            jax.ShapeDtypeStruct((seq, wide), F32),
            jax.ShapeDtypeStruct((seq, wide), BF16),
            jax.ShapeDtypeStruct((seq, wide), BF16),
        ],
        (seq // block,),
        [
            pl.BlockSpec((HEADS, block, LANES), lambda i: (0, i, 0)),
            rows(width),
            whole(spread.shape),
            out_spec_of(packed, 0),
            out_spec_of(packed, 1),
            rows(wide),
            whole((1, wide)),
        ],
        [rows(wide)] * 4,
        scratch=[pltpu.VMEM((block, wide), BF16)],
        flops=2 * seq * wide * 3 * wide,
        moved=22_000_000,
    )(o, ct, spread, packed, packed, xp, gain)


def ffn_body(b_ref, df_ref, g_ref, u_ref, d00_ref, d01_ref, d10_ref, d11_ref,
             out_ref, db_ref, dwg_ref, dwu_ref, dwd_ref, wd_ref):
    half, s = pl.program_id(0), pl.program_id(1)
    chunk = g_ref.shape[3]

    @pl.when(s == 0)
    def _():
        for part, ref in enumerate((d00_ref, d01_ref, d10_ref, d11_ref)):
            w = ref[:, 0]
            wd_ref[:, chunk * part : chunk * (part + 1)] = w.reshape(-1, chunk)

    b, df = b_ref[...], df_ref[...]
    wg = g_ref[:, 0].reshape(-1, chunk)
    wu = u_ref[:, 0].reshape(-1, chunk)
    wd = wd_ref[pl.ds(pl.multiple_of(chunk * s, chunk), chunk), :]
    gate = mm(b, wg)
    upper = mm(b, wu)
    sig = jax.nn.sigmoid(gate)
    act = gate * sig
    z = (act * upper).astype(BF16)
    dz = mm_nt(df, wd)
    dg = (dz * upper * sig * (1.0 + gate * (1.0 - sig))).astype(BF16)
    du = (dz * act).astype(BF16)

    first = jnp.logical_and(half == 0, s == 0)

    @pl.when(first)
    def _():
        out_ref[...] = mm(z, wd)
        db_ref[...] = mm_nt(dg, wg) + mm_nt(du, wu)

    @pl.when(jnp.logical_not(first))
    def _():
        out_ref[...] += mm(z, wd)
        db_ref[...] += mm_nt(dg, wg) + mm_nt(du, wu)

    dwg_ref[0, 0] = mm_tn(b, dg).astype(BF16).reshape(dwg_ref.shape[2:])
    dwu_ref[0, 0] = mm_tn(b, du).astype(BF16).reshape(dwu_ref.shape[2:])
    dwd = mm_tn(z, df).astype(BF16)
    for part in range(4):
        dwd_ref[part] = dwd[:, chunk * part : chunk * (part + 1)]


def feed_forward(b, df, packed):
    seq, wide = b.shape
    blocks = packed.shape[0]
    halves, chunks, chunk = 2, 5, 256
    hidden = halves * chunks * chunk
    gate = pl.BlockSpec((blocks, 1, 64, chunk), lambda h, s: (0, h, s, 0))
    upper = pl.BlockSpec((blocks, 1, 64, chunk), lambda h, s: (0, h, chunks + s, 0))
    down = lambda j, q: pl.BlockSpec((blocks // 2, 1, 160, chunk), lambda h, s: (h, j, 4 + q, 0))
    return call(
        ffn_body,
        [
            jax.ShapeDtypeStruct((seq, wide), F32),
            jax.ShapeDtypeStruct((seq, wide), F32),
            jax.ShapeDtypeStruct((halves, chunks, blocks, 64, chunk), BF16),
            jax.ShapeDtypeStruct((halves, chunks, blocks, 64, chunk), BF16),
            jax.ShapeDtypeStruct((4, hidden, chunk), BF16),
        ],
        (halves, chunks),
        [whole(b.shape), whole(df.shape), gate, upper, down(0, 0), down(0, 1), down(1, 0), down(1, 1)],
        [
            whole((seq, wide)),
            whole((seq, wide)),
            pl.BlockSpec((1, 1, blocks, 64, chunk), lambda h, s: (h, s, 0, 0, 0)),
            pl.BlockSpec((1, 1, blocks, 64, chunk), lambda h, s: (h, s, 0, 0, 0)),
            pl.BlockSpec((4, chunk, chunk), lambda h, s: (0, h * chunks + s, 0)),
        ],
        scratch=[pltpu.VMEM((chunks * chunk, wide), BF16)],
        flops=18 * seq * wide * hidden,
        moved=50_000_000,
    )(b, df, *([packed] * 6))


def post_body(width, m_ref, acc_ref, db_ref, df_ref, gain_ref, e_ref, wo0_ref, wo1_ref, o_ref, op_ref,
              out_ref, em_ref, do_ref, dwo_ref, dgain_ref, nat_ref, dwo_acc):
    i = pl.program_id(0)
    m, db = m_ref[...], db_ref[...]
    out_ref[...] = mm_nt((m + acc_ref[...]).astype(BF16), e_ref[:width, :]).astype(BF16)
    scale = lax.rsqrt(jnp.sum(m * m, axis=-1, keepdims=True) / width + EPSILON)
    n = m * scale
    c = db * gain_ref[...]
    mean = jnp.sum(c * n, axis=-1, keepdims=True) / width
    em = df_ref[...].astype(F32) + scale * (c - n * mean)
    em_ref[...] = em
    da = em.astype(BF16)
    dgain = jnp.sum(db * n, axis=0, keepdims=True)
    dwo = mm_tn(op_ref[...], da)

    @pl.when(i == 0)
    def _():
        dgain_ref[...] = dgain
        dwo_acc[...] = dwo

    @pl.when(i > 0)
    def _():
        dgain_ref[...] += dgain
        dwo_acc[...] += dwo

    @pl.when(i == pl.num_programs(0) - 1)
    def _():
        for part in range(4):
            w = dwo_acc[:, 256 * part : 256 * (part + 1)].astype(BF16)
            dwo_ref[part] = w.reshape(dwo_ref.shape[1:])

    dop = 0.0
    for part in range(4):
        w = columns_of((wo0_ref, wo1_ref), part)
        dop = dop + mm_nt(da[:, 256 * part : 256 * (part + 1)], w)
    nat_ref[...] = mm_nt(dop.astype(BF16), e_ref[...])
    lane = lane_of(m.shape[0])
    low = lane < HEAD
    for head in range(HEADS):
        val = nat_ref[:, LANES * (head // 2) : LANES * (head // 2 + 1)]
        if head % 2:
            val = pltpu.roll(val, 64, 1)
        val = jnp.where(low, val, 0.0)
        delta = jnp.sum(val * o_ref[head].astype(F32), axis=-1, keepdims=True)
        do_ref[head] = put_terms(val, delta, lane, HEAD).astype(BF16)


def after(m, acc, db, df, gain, spread, packed, o, op, width, block=256):
    seq, wide = m.shape
    blocks = packed.shape[0]
    rows = lambda n: pl.BlockSpec((block, n), lambda i: (i, 0))
    heads = pl.BlockSpec((HEADS, block, LANES), lambda i: (0, i, 0))
    return call(
        functools.partial(post_body, width),
        [
            jax.ShapeDtypeStruct((seq, width), BF16),
            jax.ShapeDtypeStruct((seq, wide), F32),
            jax.ShapeDtypeStruct((HEADS, seq, LANES), BF16),
            jax.ShapeDtypeStruct((4, blocks, wide // blocks, 256), BF16),
            jax.ShapeDtypeStruct((1, wide), F32),
        ],
        (seq // block,),
        [rows(wide)] * 4
        + [whole((1, wide)), whole(spread.shape), out_spec_of(packed, 0), out_spec_of(packed, 1), heads, rows(wide)],
        [
            rows(width),
            rows(wide),
            heads,
            whole((4, blocks, wide // blocks, 256)),
            whole((1, wide)),
        ],
        scratch=[pltpu.VMEM((block, wide), F32), pltpu.VMEM((wide, wide), F32)],
        flops=2 * seq * wide * 4 * wide,
        moved=35_000_000,
    )(m, acc, db, df, gain, spread, packed, packed, o, op)


def last_body(width, dq_ref, dk_ref, dv_ref, w_ref, a_ref, xp_ref, em_ref, gain_ref, e_ref,
              gi_ref, dw_ref, dgain_ref, flat_ref, dw_acc):
    i = pl.program_id(0)
    heads = HEADS + KV_HEADS
    pairs_to(flat_ref, lambda h: dq_ref[h] if h < HEADS else dk_ref[h - HEADS], heads)
    pairs_to(flat_ref, lambda h: dv_ref[h], KV_HEADS, heads * HEAD)
    flat = flat_ref[...]
    dw = mm_tn(a_ref[...], flat)
    da = mm_nt(flat, w_ref[...])
    xp = xp_ref[...].astype(F32)
    scale = lax.rsqrt(jnp.sum(xp * xp, axis=-1, keepdims=True) / width + EPSILON)
    n = xp * scale
    c = da * gain_ref[...]
    mean = jnp.sum(c * n, axis=-1, keepdims=True) / width
    grad = em_ref[...] + scale * (c - n * mean)
    dgain = jnp.sum(da * n, axis=0, keepdims=True)

    @pl.when(i == 0)
    def _():
        dgain_ref[...] = dgain
        dw_acc[...] = dw

    @pl.when(i > 0)
    def _():
        dgain_ref[...] += dgain
        dw_acc[...] += dw

    @pl.when(i == pl.num_programs(0) - 1)
    def _():
        dw_ref[...] = dw_acc[...].astype(BF16)

    e = e_ref[:width, :]
    high = grad.astype(BF16)
    gi_ref[...] = mm_nt(high, e) + mm_nt((grad - high.astype(F32)).astype(BF16), e)


def last(dq, dk, dv, w_qkv, a, xp, em, gain, spread, width, block=256):
    seq, wide = a.shape
    rows = lambda n: pl.BlockSpec((block, n), lambda i: (i, 0))
    heads = lambda n: pl.BlockSpec((n, block, LANES), lambda i: (0, i, 0))
    return call(
        functools.partial(last_body, width),
        [
            jax.ShapeDtypeStruct((seq, width), F32),
            jax.ShapeDtypeStruct((wide, QKV_PAD), BF16),
            jax.ShapeDtypeStruct((1, wide), F32),
        ],
        (seq // block,),
        [heads(HEADS), heads(KV_HEADS), heads(KV_HEADS), whole(w_qkv.shape), rows(wide), rows(wide), rows(wide)]
        + [whole((1, wide)), whole(spread.shape)],
        [rows(width), whole((wide, QKV_PAD)), whole((1, wide))],
        scratch=[pltpu.VMEM((block, QKV_PAD), BF16), pltpu.VMEM((wide, QKV_PAD), F32)],
        flops=4 * seq * wide * (QKV_PAD + width),
        moved=30_000_000,
    )(dq, dk, dv, w_qkv, a, xp, em, gain, spread)


def spread_matrix(width, blocks, wide):
    row = jnp.arange(wide, dtype=jnp.int32)
    per, step = width // blocks, wide // blocks
    place = (row // per) * step + row % per
    hit = (place[:, None] == jnp.arange(wide, dtype=jnp.int32)[None, :]) & (row < width)[:, None]
    return hit.astype(BF16)


def tables(positions, segments):
    lane = jnp.arange(LANES, dtype=jnp.int32)
    frequency = 10000.0 ** (-((lane % 32).astype(F32) * 2.0 / HEAD))
    angles = positions.astype(F32)[:, None] * frequency[None, :]
    cos, sin = jnp.cos(angles), jnp.sin(angles)
    high = (lane % HEAD >= 32)[None, :]
    sa = jnp.where(high, sin, 0.0)
    sb = jnp.where(high, 0.0, -sin)
    doc = (lane - HEAD)[None, :]
    mine = segments[:, None] == doc
    in_doc = (doc >= 0) & (doc < DOCS)
    aq = jnp.where(mine & in_doc, MASKED, 0.0)
    ak = jnp.where(in_doc & ~mine, 1.0, 0.0)
    ak = jnp.where((doc >= DOCS) & (doc < DOCS + 3), -1.0, ak)
    return cos, sa, sb, aq, ak


def layer(x, ct, segments, positions, w_qkv, get_packed, gain_attn, gain_ffn, spread, reduce_first):
    width = x.shape[1]
    cos, sa, sb, aq, ak = tables(positions, segments)
    xp, a, q, k, v = pre_attention(x, spread, w_qkv, gain_attn, cos, sa, sb, aq, ak)
    o, q2 = attend(q, k, v)
    packed = get_packed
    op, m, b, df = middle(o, ct, spread, packed, xp, gain_ffn)
    acc, db, dwg, dwu, dwd = feed_forward(b, df, packed)
    out, em, do, dwo, dgain_ffn = after(m, acc, db, df, gain_ffn, spread, packed, o, op, width)
    first = reduce_first(dwg, dwu, dwd, dwo)
    dq, dk, dv = attend_back(q2, k, v, do, cos, sa, sb)
    gi, dw, dgain_attn = last(dq, dk, dv, w_qkv, a, xp, em, gain_attn, spread, width)
    return out, gi, first, dw, dgain_attn, dgain_ffn


def pad_rows(w, blocks, step=64):
    per = w.shape[0] // blocks
    return jnp.pad(w.reshape(blocks, per, w.shape[1]), ((0, 0), (0, step - per), (0, 0)))


def pad_cols(w, blocks, step=64):
    per = w.shape[1] // blocks
    w = jnp.pad(w.reshape(w.shape[0], blocks, per), ((0, 0), (0, 0), (0, step - per)))
    return w.reshape(w.shape[0], blocks * step)


def cut_rows(w, per):
    return w[:, :per].reshape(w.shape[0] * per, w.shape[2])


def cut_cols(w, per, step=64):
    blocks = w.shape[1] // step
    return w.reshape(w.shape[0], blocks, step)[:, :, :per].reshape(w.shape[0], blocks * per)


def chunked(w, chunk=256):
    blocks, rows, cols = w.shape
    w = w.reshape(blocks, rows, cols // chunk, chunk).transpose(0, 2, 1, 3)
    return w.reshape(blocks, cols // chunk * rows, chunk)


def joined(w, rows):
    blocks, total, chunk = w.shape
    w = w.reshape(blocks, total // rows, rows, chunk).transpose(0, 2, 1, 3)
    return w.reshape(blocks, rows, total // rows * chunk)


def pack_half(w_gate, w_up, w_down, w_out, blocks, groups):
    down = pad_cols(w_down, groups)
    down = down.reshape(blocks, w_down.shape[0] // blocks, down.shape[1])
    return jnp.concatenate(
        [
            chunked(pad_rows(w_gate, blocks)),
            chunked(pad_rows(w_up, blocks)),
            chunked(down),
            chunked(pad_rows(pad_cols(w_out, groups), blocks)),
        ],
        axis=1,
    )


def add(left, right):
    return (left.astype(F32) + right.astype(F32)).astype(BF16)


def swap(x):
    return lax.ppermute(x, "ctx", [(0, 1), (1, 0)])


def across(x, bit, count):
    return lax.ppermute(x, "dp", [(i, i ^ (1 << bit)) for i in range(count)])


def pick(x, index, axis=0):
    return lax.dynamic_index_in_dim(x, index, axis, keepdims=False)


def in_order(own, other, index):
    return jnp.where(index == 0, jnp.stack([own, other]), jnp.stack([other, own]))


def gather_projections(shard, bits):
    count = 1 << len(bits)
    grow = lambda buf, bit: in_order(buf, across(buf, bit, count), bits[bit])
    buf = grow(grow(shard, 2), 3)
    half = shard.shape[0] // 2
    first = grow(grow(buf[:, :, :half], 0), 1)
    second = grow(grow(buf[:, :, half:], 1), 0)
    first = first.transpose(2, 3, 0, 1, 4, 5).reshape(count, half, -1)
    second = second.transpose(2, 3, 1, 0, 4, 5).reshape(count, half, -1)
    return jnp.concatenate([first, second], axis=1)


def reduce_rows(first, second, bits):
    count = 1 << len(bits)
    cube = (2,) * len(bits)

    def step(buf, bit, axis):
        got = across(pick(buf, 1 - bits[bit], axis), bit, count)
        return add(pick(buf, bits[bit], axis), got)

    first = step(step(first.reshape(cube + first.shape[1:]), 0, 3), 1, 2)
    second = step(step(second.reshape(cube + second.shape[1:]), 1, 2), 0, 2)
    both = jnp.stack([first, second], axis=2)
    return step(step(both, 3, 0), 2, 0)


def shards_of_two(inputs, segment_ids, positions, w_query, w_key, w_value, w_out, w_gate, w_up,
                  w_down, gain_attn, gain_ffn, cotangent):
    count = lax.axis_size("dp")
    me, core = lax.axis_index("dp"), lax.axis_index("ctx")
    bits = [(me >> bit) & 1 for bit in range(count.bit_length() - 1)]
    per = gain_attn.shape[0]
    width = per * count
    groups = w_out.shape[1] // per
    hidden = w_down.shape[0]
    n_q, n_k = w_query.shape[1], w_key.shape[1]
    n_qkv = n_q + 2 * n_k

    shard = jnp.concatenate(
        [w_query, w_key, w_value, gain_attn[:, None], gain_ffn[:, None]], axis=1
    )
    shard = jnp.pad(shard, ((0, 64 - per), (0, 896 - n_qkv - 2)))
    mine = gather_projections(shard, bits)
    packed = pack_half(w_gate, w_up, w_down, w_out, 1, groups)[0]
    packed = lax.all_gather(packed, ("dp", "ctx"), axis=0, tiled=False)
    packed = packed.reshape((count, 2) + packed.shape[1:])

    pair = in_order(mine, swap(mine), core).reshape(2, count * 64, 896)
    cut = lambda a, b: [pair[0, :, a:b], pair[1, :, a:b]]
    w_qkv = jnp.concatenate(
        cut(0, n_q) + cut(n_q, n_q + n_k) + cut(n_q + n_k, n_qkv)
        + [jnp.zeros((count * 64, QKV_PAD - QKV), BF16)],
        axis=1,
    )
    gains = mine[:, :, n_qkv : n_qkv + 2].astype(F32).reshape(count * 64, 2).T

    def sequence(x):
        own, other = pick(x[:, 0], core), swap(pick(x[:, 0], 1 - core))
        return in_order(own, other, core).reshape(-1, x.shape[3])

    x, ct = sequence(inputs), sequence(cotangent)

    def sum_first(dwg, dwu, dwd, dwo):
        def core_sum(t):
            return add(pick(t, core), swap(pick(t, 1 - core)))

        g, u = core_sum(dwg), core_sum(dwu)
        d = core_sum(dwd.reshape(2, 2, count, hidden, 256))
        o = core_sum(dwo.reshape((2, 2) + dwo.shape[1:]))
        flat = lambda t: t.transpose(1, 0, 2, 3).reshape(count, -1, 256)
        return reduce_rows(
            jnp.concatenate([flat(g), d[0], o[0]], axis=1),
            jnp.concatenate([flat(u), d[1], o[1]], axis=1),
            bits,
        )

    out, gi, first, dw, dga, dgf = layer(
        x, ct, pick(segment_ids[:, 0], core), pick(positions[:, 0], core),
        w_qkv, packed, gains[:1], gains[1:], spread_matrix(width, count, count * 64), sum_first,
    )

    def part_of(j):
        cols = lambda a, n: dw[:, a + n * j : a + n * (j + 1)]
        parts = [cols(0, n_q), cols(2 * n_q, n_k), cols(2 * (n_q + n_k), n_k)]
        parts += [dga.astype(BF16).T, dgf.astype(BF16).T]
        part = jnp.concatenate(parts, axis=1)
        return jnp.pad(part, ((0, 0), (0, 896 - part.shape[1]))).reshape(count, 64, 896)

    both = jnp.stack([part_of(0), part_of(1)])
    total = add(pick(both, core), swap(pick(both, 1 - core)))
    last_sum = reduce_rows(total[:, :32], total[:, 32:], bits)
    last_sum = last_sum.reshape(64, 896)[:per].astype(F32)

    def tokens(seq):
        halves = seq.reshape(2, seq.shape[0] // 2, seq.shape[1])
        own, other = pick(halves, core), swap(pick(halves, 1 - core))
        return in_order(own, other, core)[:, None]

    rows = 5 * 64
    gate = joined(first[:1, :rows], 64)[0, :per]
    upper = joined(first[1:, :rows], 64)[0, :per]
    down = first[:, rows : rows + hidden].transpose(1, 0, 2).reshape(hidden, -1)
    outer = first[:, rows + hidden :].transpose(1, 0, 2).reshape(64, -1)[:per]
    return (
        tokens(out),
        tokens(gi),
        last_sum[:, :n_q],
        last_sum[:, n_q : n_q + n_k],
        last_sum[:, n_q + n_k : n_qkv],
        cut_cols(outer.astype(F32), per),
        gate.astype(F32),
        upper.astype(F32),
        cut_cols(down.astype(F32), per),
        last_sum[:, n_qkv],
        last_sum[:, n_qkv + 1],
    )


def shards_of_many(inputs, segment_ids, positions, w_query, w_key, w_value, w_out, w_gate, w_up,
                   w_down, gain_attn, gain_ffn, cotangent):
    count, cores = lax.axis_size("dp"), lax.axis_size("ctx")
    core = lax.axis_index("ctx")
    share = cores // MICRO
    per = gain_attn.shape[0]
    width = per * count

    def gathered(w):
        return lax.all_gather(lax.all_gather(w, "dp", axis=0, tiled=True), "ctx", axis=1, tiled=True)

    full = [gathered(w) for w in (w_query, w_key, w_value, w_out, w_gate, w_up, w_down)]
    gain_pair = lax.all_gather(jnp.stack([gain_attn, gain_ffn]), "dp", axis=1, tiled=True)
    gains = pad_cols(gain_pair.astype(F32), count)
    w_qkv = pad_rows(jnp.concatenate(full[:3], axis=1), count).reshape(count * 64, QKV)
    w_qkv = jnp.pad(w_qkv, ((0, 0), (0, QKV_PAD - QKV)))
    w_o, w_g, w_u, w_d = full[3:]
    half = lambda w, j: w[:, w.shape[1] // 2 * j : w.shape[1] // 2 * (j + 1)]
    packed = jnp.stack(
        [pack_half(half(w_g, j), half(w_u, j), half(w_d, j), half(w_o, j), count, count // 2) for j in range(2)],
        axis=1,
    )
    which = core // share
    sequence = lambda x: pick(lax.all_gather(x[:, 0], "ctx", axis=1, tiled=True), which)
    out, gi, first, dw, dga, dgf = layer(
        sequence(inputs), sequence(cotangent),
        pick(segment_ids[:, 0], which), pick(positions[:, 0], which),
        w_qkv, packed, gains[:1], gains[1:], spread_matrix(width, count, count * 64), lambda *t: t,
    )
    dwg, dwu, dwd, dwo = first
    wide_of = lambda t: jnp.concatenate(
        [cut_rows(t[j].transpose(1, 2, 0, 3).reshape(count, 64, -1), per) for j in range(2)], axis=1
    )
    side = lambda t: jnp.concatenate([t[q] for q in range(4)], axis=-1)
    d_qkv = cut_rows(dw.reshape(count, 64, QKV_PAD), per)
    n_q, n_k = HEADS * HEAD, KV_HEADS * HEAD
    grads = [
        d_qkv[:, :n_q],
        d_qkv[:, n_q : n_q + n_k],
        d_qkv[:, n_q + n_k : QKV],
        cut_cols(cut_rows(side(dwo), per), per),
        wide_of(dwg),
        wide_of(dwu),
        cut_cols(side(dwd), per),
    ]

    def summed(g):
        g = lax.psum_scatter(g * (1.0 / share), "dp", scatter_dimension=0, tiled=True)
        return lax.psum_scatter(g, "ctx", scatter_dimension=1, tiled=True).astype(F32)

    sums = [summed(g.astype(BF16)) for g in grads]
    dgain = cut_cols(jnp.concatenate([dga, dgf]), per) * (1.0 / share)
    dgain = lax.psum_scatter(lax.psum(dgain, "ctx"), "dp", scatter_dimension=1, tiled=True)

    def tokens(seq):
        rows = seq.shape[0] // cores
        every = lax.all_gather(seq, "ctx", axis=0, tiled=False)
        return lax.dynamic_slice_in_dim(every[::share], core * rows, rows, axis=1)[:, None]

    return (tokens(out), tokens(gi), *sums, dgain[0], dgain[1])


def solution(mesh):
    two = mesh.shape["ctx"] == MICRO and mesh.shape["dp"] == 16
    matrices = (P("dp", "ctx"),) * 7 + (P("dp"), P("dp"))
    tokens = P(None, "dp", "ctx", None)
    return jax.shard_map(
        shards_of_two if two else shards_of_many,
        mesh=mesh,
        in_specs=(tokens, P(None, "dp", None), P(None, "dp", None)) + matrices + (tokens,),
        out_specs=(tokens, tokens) + matrices,
        check_vma=False,
    )
```

time: 1240 us -> 565 us (0.46)
  blocking collectives: 613 us -> 0 us
  matrix products: 334 us -> 0 us
  Pallas kernels: 0 us -> 195 us
  waiting for transfers between devices: 81.4 us -> 165 us
  starting transfers between devices: 14.2 us -> 29 us
    unnamed x4 -> x0, blocking collectives: 497 us -> none
    dot_general x112 -> x0, matrix products: 334 us -> none  [the longest x14 66 us: outer_cols(): lax.dot_general(left, right, (((1,), (1,)), ((), ())), preferred_element_...]
    pallas_call x0 -> x7, Pallas kernels: none -> 195 us  [the longest x1 62.3 us: feed_forward(): call(ffn_body, [jax.ShapeDtypeStruct((seq, wide), F32), jax.ShapeDtypeStr...]
    ppermute x0 -> x28, waiting for transfers between devices: none -> 165 us  [the longest x18 165 us: across(): return lax.ppermute(x, 'dp', [(i, i ^ 1 << bit) for i in range(count)])]
    all_gather x13 -> x0, blocking collectives: 115 us -> none  [the longest x1 46.1 us: fetch_weights(): lax.all_gather(wide_shards[2], 'dp', axis=0, tiled=True)]
    all_gather x5 -> x1, waiting for transfers between devices: 80.4 us -> 0.01 us  [shards_of_two(): packed = lax.all_gather(packed, ('dp', 'ctx'), axis=0, tiled=False)]
    unnamed x241 -> x72, local copies, waits for them, and re-layouts: 80.5 us -> 3.84 us
    ppermute x0 -> x28, starting transfers between devices: none -> 29 us  [the longest x18 27 us: across(): return lax.ppermute(x, 'dp', [(i, i ^ 1 << bit) for i in range(count)])]
  transfers between devices with their start and end apart: 23 -> 29, of which waited for: 2 -> 10; matrix products, arithmetic and copies ran while one was open for 63% -> 25% of each run, Pallas kernels for 0% -> 22%
where the time goes in v1:
time: 565 us; the launch traced here: 561 us
  Pallas kernels  195 us (35%)
  waiting for transfers between devices  165 us (29%)
  local copies, waits for them, and re-layouts  92.6 us (16%)
  other arithmetic  63.5 us (11%)
  starting transfers between devices  29 us (5%)
  between operations  15.4 us (3%)
    ppermute x18, waiting for transfers between devices, across(): return lax.ppermute(x, 'dp', [(i, i ^ 1 << bit) for i in range(count)])  165 us
    pallas_call x1, Pallas kernels, feed_forward(): call(ffn_body, [jax.ShapeDtypeStruct((seq, wide), F32), jax.ShapeDtypeStr...  62.3 us
    pallas_call x1, Pallas kernels, attend_back(): call(functools.partial(attend_back_body, block), [jax.ShapeDtypeStruct(q....  35.5 us
    ppermute x18, starting transfers between devices, across(): return lax.ppermute(x, 'dp', [(i, i ^ 1 << bit) for i in range(count)])  27 us
    pallas_call x1, Pallas kernels, attend(): call(functools.partial(attend_body, block), [shape, shape], (KV_HEADS,),...  25.4 us
    pallas_call x1, Pallas kernels, after(): call(functools.partial(post_body, width), [jax.ShapeDtypeStruct((seq, wid...  24.1 us
    pallas_call x1, Pallas kernels, last(): call(functools.partial(last_body, width), [jax.ShapeDtypeStruct((seq, wid...  22.7 us
    convert_element_type x11, other arithmetic, add(): return (left.astype(F32) + right.astype(F32)).astype(BF16)  16.7 us
  transfers between devices with their start and end apart: 29, of which 10 were waited for; matrix products, arithmetic and copies ran while one was open for 25% of the time, Pallas kernels for 22%

profile of v1, /device:TPU:0, one launch (start us, length us, event | category | flops | bytes accessed | tf_op | source)
XLA Modules:
  0.0 561.0 jit_solution(8443152254076713399)
XLA Ops:
  21.3 20.4 %collective-permute-done.2 = bf16[2,64,896]{2,1,0:T(8,128)(2,1)S(1)} collective-permute-done((bf16[2,64,896]{2,1,0:T(8,128)(2,1)S(1)}, bf16[2,64,896]{2,1,0:T(8,128)(2,1)S(1)}, u32[]{:S(2)}, u32[]{:S(2)}) %collective-permute-start.2) | collective-permute-done | bytes 229408 | tf_op jit(solution)/shard_map/ppermute | solution.py:608
  45.1 4.4 collective-permute-done.3
  53.1 16.2 %collective-permute-done.4 = bf16[2,2,2,32,896]{4,3,0,2,1:T(8,128)(2,1)S(1)} collective-permute-done((bf16[2,2,2,32,896]{4,3,0,2,1:T(8,128)(2,1)S(1)}, bf16[2,2,2,32,896]{4,3,0,2,1:T(8,128)(2,1)S(1)}, u32[]{:S(2)}, u32[]{:S(2)}) %collective-permute-start.4) | collective-permute-done | bytes 458784 | tf_op jit(solution)/shard_map/ppermute | solution.py:608
  69.4 4.8 copy.167
  75.6 4.5 copy.168
  80.2 7.0 %pad_maximum_fusion.2 = bf16[16,64,896]{1,0,2:T(8,128)(2,1)} fusion(bf16[16,32,896]{1,0,2:T(8,128)(2,1)} %copy.168, bf16[16,32,896]{1,0,2:T(8,128)(2,1)} %copy.167), kind=kLoop, calls=%fused_computation.24 | loop fusion | flops 3670016 | bytes 3670016 | tf_op jit(solution)/shard_map/concatenate | solution.py:628
  87.2 5.3 copy.169
  114.7 6.4 %concatenate.112.w_ref = bf16[1024,1664]{1,0:T(8,128)(2,1)} concatenate(bf16[1024,480]{1,0:T(8,128)(2,1)S(1)} %get-tuple-element.74, bf16[1024,480]{1,0:T(8,128)(2,1)S(1)} %get-tuple-element.73, bf16[1024,160]{1,0:T(8,128)(2,1)} %get-tuple-element.72, bf16[1024,160]{1,0:T(8,128)(2,1)} %get-tuple-element.71, bf16[1024,160]{1,0:T(8,128)(2,1)S(1)} %get-tuple-element.70, ...), dimensions={1} | concatenate | bytes 6815744 | tf_op jit(solution)/shard_map/concatenate | solution.py:668
  121.0 13.6 %shard_map.212 = (bf16[1024,1024]{1,0:T(8,128)(2,1)}, bf16[1024,1024]{1,0:T(8,128)(2,1)}, bf16[15,1024,128]{2,1,0:T(8,128)(2,1)}, bf16[5,1024,128]{2,1,0:T(8,128)(2,1)}, bf16[5,1024,128]{2,1,0:T(8,128)(2,1)}) custom-call(bf16[1024,960]{1,0:T(8,128)(2,1)} %bitcast.269, bf16[1024,1024]{1,0:T(8,128)(2,1)} %fusion.6.e_ref, ...), custom_call_target="tpu_custom_call" | custom-call | flops 5502926848 | bytes 20000000 | tf_op jit(solution)/shard_map/pallas_call | solution.py:116
  134.7 25.4 %shard_map.213 = (bf16[15,1024,128]{2,1,0:T(8,128)(2,1)}, bf16[15,1024,128]{2,1,0:T(8,128)(2,1)}) custom-call(bf16[15,1024,128]{2,1,0:T(8,128)(2,1)} %get-tuple-element.38.q_ref, bf16[5,1024,128]{2,1,0:T(8,128)(2,1)} %get-tuple-element.39.k_ref, bf16[5,1024,128]{2,1,0:T(8,128)(2,1)} %get-tuple-element.40.v_ref), custom_call_target="tpu_custom_call" | custom-call | flops 8053063680 | bytes 15000000 | tf_op jit(solution)/shard_map/pallas_call | solution.py:166
  160.0 11.4 %shard_map.214 = (bf16[1024,1024]{1,0:T(8,128)(2,1)}, f32[1024,1024]{1,0:T(8,128)}, bf16[1024,1024]{1,0:T(8,128)(2,1)}, bf16[1024,1024]{1,0:T(8,128)(2,1)}) custom-call(bf16[15,1024,128]{2,1,0:T(8,128)(2,1)} %get-tuple-element.41.o_ref, bf16[1024,960]{1,0:T(8,128)(2,1)} %bitcast.248, bf16[1024,1024]{1,0:T(8,128)(2,1)} %fusion.6.e_ref, ...), custom_call_target="tpu_custom_call" | custom-call | flops 6442450944 | bytes 22000000 | tf_op jit(solution)/shard_map/pallas_call | solution.py:279
  171.5 62.3 %shard_map.215 = (f32[1024,1024]{1,0:T(8,128)}, f32[1024,1024]{1,0:T(8,128)}, bf16[2,5,16,64,256]{4,3,2,1,0:T(8,128)(2,1)}, bf16[2,5,16,64,256]{4,3,2,1,0:T(8,128)(2,1)}, bf16[4,2560,256]{2,1,0:T(8,128)(2,1)}) custom-call(bf16[1024,1024]{1,0:T(8,128)(2,1)} %get-tuple-element.44.b_ref, bf16[1024,1024]{1,0:T(8,128)(2,1)} %get-tuple-element.45.df_ref, ...), custom_call_target="tpu_custom_call" | custom-call | flops 48318382080 | bytes 50000000 | tf_op jit(solution)/shard_map/pallas_call | solution.py:355
  239.7 24.1 %shard_map.216 = (bf16[1024,960]{1,0:T(8,128)(2,1)}, f32[1024,1024]{1,0:T(8,128)}, bf16[15,1024,128]{2,1,0:T(8,128)(2,1)}, bf16[4,16,64,256]{3,2,1,0:T(8,128)(2,1)}, f32[1,1024]{1,0:T(1,128)}) custom-call(f32[1024,1024]{1,0:T(8,128)} %get-tuple-element.43.m_ref, f32[1024,1024]{1,0:T(8,128)} %get-tuple-element.46.acc_ref, ...), custom_call_target="tpu_custom_call" | custom-call | flops 8589934592 | bytes 35000000 | tf_op jit(solution)/shard_map/pallas_call | solution.py:431
  270.3 35.5 %shard_map.217 = (bf16[15,1024,128]{2,1,0:T(8,128)(2,1)}, bf16[5,1024,128]{2,1,0:T(8,128)(2,1)}, bf16[5,1024,128]{2,1,0:T(8,128)(2,1)}) custom-call(bf16[15,1024,128]{2,1,0:T(8,128)(2,1)} %get-tuple-element.50.q_ref, bf16[5,1024,128]{2,1,0:T(8,128)(2,1)} %get-tuple-element.39.k_ref, bf16[5,1024,128]{2,1,0:T(8,128)(2,1)} %get-tuple-element.40.v_ref, ...), custom_call_target="tpu_custom_call" | custom-call | flops 20132659200 | bytes 20000000 | tf_op jit(solution)/shard_map/pallas_call | solution.py:225
  305.8 22.7 %shard_map.218 = (f32[1024,960]{1,0:T(8,128)}, bf16[1024,1664]{1,0:T(8,128)(2,1)}, f32[1,1024]{1,0:T(1,128)}) custom-call(bf16[15,1024,128]{2,1,0:T(8,128)(2,1)} %get-tuple-element.52.dq_ref, bf16[5,1024,128]{2,1,0:T(8,128)(2,1)} %get-tuple-element.53.dk_ref, bf16[5,1024,128]{2,1,0:T(8,128)(2,1)} %get-tuple-element.54.dv_ref, ...), custom_call_target="tpu_custom_call" | custom-call | flops 11005853696 | bytes 30000000 | tf_op jit(solution)/shard_map/pallas_call | solution.py:496
  330.1 3.9 fusion.62
  336.7 4.8 concatenate.115
  343.4 4.4 concatenate.114
  387.3 37.9 %collective-permute-done.14 = bf16[2,2,2,32,896]{4,3,1,0,2:T(8,128)(2,1)} collective-permute-done((bf16[2,2,2,32,896]{4,3,1,0,2:T(8,128)(2,1)}, bf16[2,2,2,32,896]{4,3,1,0,2:T(8,128)(2,1)}, u32[]{:S(2)}, u32[]{:S(2)}) %collective-permute-start.14) | collective-permute-done | bytes 458784 | tf_op jit(solution)/shard_map/ppermute | solution.py:608
  444.9 22.6 %collective-permute-done.13 = bf16[2,2,32,896]{3,2,1,0:T(8,128)(2,1)S(1)} collective-permute-done((bf16[2,2,32,896]{3,2,1,0:T(8,128)(2,1)S(1)}, bf16[2,2,32,896]{3,2,1,0:T(8,128)(2,1)S(1)}, u32[]{:S(2)}, u32[]{:S(2)}) %collective-permute-start.13) | collective-permute-done | bytes 229408 | tf_op jit(solution)/shard_map/ppermute | solution.py:608
  477.0 3.8 maximum_select_fusion.4
  480.9 46.5 %collective-permute-done.16 = bf16[2,2,32,896]{3,2,1,0:T(8,128)(2,1)} collective-permute-done((bf16[2,2,32,896]{3,2,1,0:T(8,128)(2,1)}, bf16[2,2,32,896]{3,2,1,0:T(8,128)(2,1)}, u32[]{:S(2)}, u32[]{:S(2)}) %collective-permute-start.16) | collective-permute-done | bytes 229408 | tf_op jit(solution)/shard_map/ppermute | solution.py:608
  528.5 4.8 maximum_select_fusion
  539.0 10.5 %collective-permute-done.27 = bf16[2,544,256]{2,1,0:T(8,128)(2,1)S(1)} collective-permute-done((bf16[2,544,256]{2,1,0:T(8,128)(2,1)S(1)}, bf16[2,544,256]{2,1,0:T(8,128)(2,1)S(1)}, u32[]{:S(2)}, u32[]{:S(2)}) %collective-permute-start.27) | collective-permute-done | bytes 557088 | tf_op jit(solution)/shard_map/ppermute | solution.py:608
  (259 shorter events, 142.3 us)
Async XLA Ops:
  7.2 152.8 %all-gather.2.cloned.1.call-start = ((), (), s32[]{:S(2)}) async-start(), calls=%async_computation | async-start | bytes 18382848 | tf_op jit(solution)/shard_map/all_gather | solution.py:663
  16.6 82.4 %collective-permute-start = (bf16[512,960]{0,1:T(8,128)(2,1)}, bf16[512,960]{0,1:T(8,128)(2,1)}, u32[]{:S(2)}, u32[]{:S(2)}) collective-permute-start(bf16[512,960]{0,1:T(8,128)(2,1)} %get-tuple-element.88), channel_id=1, source_target_pairs={{0,1},{1,0},{2,3},{3,2},{4,5},{5,4},{6,7},{7,6},{8,9},{9,8},{10,11... | collective-permute-start | bytes 2949128 | tf_op jit(solution)/shard_map/ppermute | solution.py:604
  18.5 84.9 %collective-permute-start.8 = (bf16[512,960]{0,1:T(8,128)(2,1)}, bf16[512,960]{0,1:T(8,128)(2,1)}, u32[]{:S(2)}, u32[]{:S(2)}) collective-permute-start(bf16[512,960]{0,1:T(8,128)(2,1)} %get-tuple-element.86), channel_id=1, source_target_pairs={{0,1},{1,0},{2,3},{3,2},{4,5},{5,4},{6,7},{7,6},{8,9},{9,8},{10,11... | collective-permute-start | bytes 2949128 | tf_op jit(solution)/shard_map/ppermute | solution.py:604
  18.6 23.1 %collective-permute-start.2 = (bf16[2,64,896]{2,1,0:T(8,128)(2,1)S(1)}, bf16[2,64,896]{2,1,0:T(8,128)(2,1)S(1)}, u32[]{:S(2)}, u32[]{:S(2)}) collective-permute-start(bf16[2,64,896]{2,1,0:T(8,128)(2,1)S(1)} %maximum_select_fusion.12), channel_id=1, source_target_pairs={{0,16},{2,18},{4,20},{6,22},{8,24},{10,26},{12,28},{14,30},{16,0},... | collective-permute-start | bytes 688136 | tf_op jit(solution)/shard_map/ppermute | solution.py:608
  49.6 19.7 %collective-permute-start.4 = (bf16[2,2,2,32,896]{4,3,0,2,1:T(8,128)(2,1)S(1)}, bf16[2,2,2,32,896]{4,3,0,2,1:T(8,128)(2,1)S(1)}, u32[]{:S(2)}, u32[]{:S(2)}) collective-permute-start(bf16[2,2,2,32,896]{4,3,0,2,1:T(8,128)(2,1)S(1)} %maximum_select_fusion.8), channel_id=1, source_target_pairs={{0,4},{2,6},{4,0},{6,2},{8,12},{10,14},{12,8},{14,10},{16,20},{18,... | collective-permute-start | bytes 1376264 | tf_op jit(solution)/shard_map/ppermute | solution.py:608
  51.3 22.9 %collective-permute-start.6 = (bf16[2,2,2,32,896]{4,3,2,1,0:T(8,128)(2,1)S(1)}, bf16[2,2,2,32,896]{4,3,2,1,0:T(8,128)(2,1)}, u32[]{:S(2)}, u32[]{:S(2)}) collective-permute-start(bf16[2,2,2,32,896]{4,3,2,1,0:T(8,128)(2,1)S(1)} %maximum_select_fusion.10), channel_id=1, source_target_pairs={{0,2},{2,0},{4,6},{6,4},{8,10},{10,8},{12,14},{14,12},{16,18},{18,... | collective-permute-start | bytes 1376264 | tf_op jit(solution)/shard_map/ppermute | solution.py:608
  92.6 16.6 %collective-permute-start.7 = (bf16[16,64,896]{2,1,0:T(8,128)(2,1)}, bf16[16,64,896]{2,1,0:T(8,128)(2,1)}, u32[]{:S(2)}, u32[]{:S(2)}) collective-permute-start(bf16[16,64,896]{2,1,0:T(8,128)(2,1)} %copy.169), channel_id=1, source_target_pairs={{0,1},{1,0},{2,3},{3,2},{4,5},{5,4},{6,7},{7,6},{8,9},{9,8},{10,11... | collective-permute-start | bytes 5505032 | tf_op jit(solution)/shard_map/ppermute | solution.py:604
  237.6 116.6 %collective-permute-start.23 = (bf16[5,16,64,256]{3,2,1,0:T(8,128)(2,1)}, bf16[5,16,64,256]{3,2,1,0:T(8,128)(2,1)}, u32[]{:S(2)}, u32[]{:S(2)}) collective-permute-start(bf16[5,16,64,256]{3,2,1,0:T(8,128)(2,1)} %dynamic-slice_bitcast_fusion), channel_id=1, source_target_pairs={{0,1},{1,0},{2,3},{3,2},{4,5},{5,4},{6,7},{7,6},{8,9},{9,8},{10,11... | collective-permute-start | bytes 7864328 | tf_op jit(solution)/shard_map/ppermute | solution.py:604
  239.7 117.4 %collective-permute-start.19 = (bf16[2,16,160,256]{3,2,1,0:T(8,128)(2,1)}, bf16[2,16,160,256]{3,2,1,0:T(8,128)(2,1)}, u32[]{:S(2)}, u32[]{:S(2)}) collective-permute-start(bf16[2,16,160,256]{3,2,1,0:T(8,128)(2,1)} %dynamic-slice_bitcast_fusion.1), channel_id=1, source_target_pairs={{0,1},{1,0},{2,3},{3,2},{4,5},{5,4},{6,7},{7,6},{8,9},{9,8},{10,11... | collective-permute-start | bytes 7864328 | tf_op jit(solution)/shard_map/ppermute | solution.py:604
  266.2 85.9 %collective-permute-start.20 = (bf16[2,16,64,256]{3,2,1,0:T(8,128)(2,1)}, bf16[2,16,64,256]{3,2,1,0:T(8,128)(2,1)}, u32[]{:S(2)}, u32[]{:S(2)}) collective-permute-start(bf16[2,16,64,256]{3,2,1,0:T(8,128)(2,1)} %dynamic-slice_bitcast_fusion.7), channel_id=1, source_target_pairs={{0,1},{1,0},{2,3},{3,2},{4,5},{5,4},{6,7},{7,6},{8,9},{9,8},{10,11... | collective-permute-start | bytes 3145736 | tf_op jit(solution)/shard_map/ppermute | solution.py:604
  270.3 95.2 %collective-permute-start.18 = (bf16[5,16,64,256]{3,2,1,0:T(8,128)(2,1)}, bf16[5,16,64,256]{3,2,1,0:T(8,128)(2,1)}, u32[]{:S(2)}, u32[]{:S(2)}) collective-permute-start(bf16[5,16,64,256]{3,2,1,0:T(8,128)(2,1)} %dynamic-slice_bitcast_fusion.2), channel_id=1, source_target_pairs={{0,1},{1,0},{2,3},{3,2},{4,5},{5,4},{6,7},{7,6},{8,9},{9,8},{10,11... | collective-permute-start | bytes 7864328 | tf_op jit(solution)/shard_map/ppermute | solution.py:604
  351.6 21.8 %collective-permute-start.11 = (bf16[16,64,896]{2,1,0:T(8,128)(2,1)}, bf16[16,64,896]{2,1,0:T(8,128)(2,1)}, u32[]{:S(2)}, u32[]{:S(2)}) collective-permute-start(bf16[16,64,896]{2,1,0:T(8,128)(2,1)} %fusion.15), channel_id=1, source_target_pairs={{0,1},{1,0},{2,3},{3,2},{4,5},{5,4},{6,7},{7,6},{8,9},{9,8},{10,11... | collective-permute-start | bytes 5505032 | tf_op jit(solution)/shard_map/ppermute | solution.py:604
  364.2 63.9 %collective-permute-start.24 = (bf16[2,2,2,544,256]{4,3,2,1,0:T(8,128)(2,1)}, bf16[2,2,2,544,256]{4,3,2,1,0:T(8,128)(2,1)}, u32[]{:S(2)}, u32[]{:S(2)}) collective-permute-start(bf16[2,2,2,544,256]{4,3,2,1,0:T(8,128)(2,1)} %dynamic-slice_bitcast_fusion.3), channel_id=1, source_target_pairs={{0,4},{2,6},{4,0},{6,2},{8,12},{10,14},{12,8},{14,10},{16,20},{18,... | collective-permute-start | bytes 6684680 | tf_op jit(solution)/shard_map/ppermute | solution.py:608
  371.7 59.8 %collective-permute-start.21 = (bf16[2,2,2,544,256]{4,3,2,1,0:T(8,128)(2,1)}, bf16[2,2,2,544,256]{4,3,2,1,0:T(8,128)(2,1)}, u32[]{:S(2)}, u32[]{:S(2)}) collective-permute-start(bf16[2,2,2,544,256]{4,3,2,1,0:T(8,128)(2,1)} %dynamic-slice_bitcast_fusion.4), channel_id=1, source_target_pairs={{0,2},{2,0},{4,6},{6,4},{8,10},{10,8},{12,14},{14,12},{16,18},{18,... | collective-permute-start | bytes 6684680 | tf_op jit(solution)/shard_map/ppermute | solution.py:608
  379.3 45.9 %collective-permute-start.14 = (bf16[2,2,2,32,896]{4,3,1,0,2:T(8,128)(2,1)}, bf16[2,2,2,32,896]{4,3,1,0,2:T(8,128)(2,1)}, u32[]{:S(2)}, u32[]{:S(2)}) collective-permute-start(bf16[2,2,2,32,896]{4,3,1,0,2:T(8,128)(2,1)} %bitcast.227), channel_id=1, source_target_pairs={{0,4},{2,6},{4,0},{6,2},{8,12},{10,14},{12,8},{14,10},{16,20},{18,... | collective-permute-start | bytes 1376264 | tf_op jit(solution)/shard_map/ppermute | solution.py:608
  383.5 144.9 %collective-permute-start.10 = (f32[512,960]{0,1:T(8,128)}, f32[512,960]{0,1:T(8,128)}, u32[]{:S(2)}, u32[]{:S(2)}) collective-permute-start(f32[512,960]{0,1:T(8,128)} %bitcast.272), channel_id=1, source_target_pairs={{0,1},{1,0},{2,3},{3,2},{4,5},{5,4},{6,7},{7,6},{8,9},{9,8},{10,11... | collective-permute-start | bytes 5898248 | tf_op jit(solution)/shard_map/ppermute | solution.py:604
  386.6 90.4 %collective-permute-start.9 = (bf16[512,960]{0,1:T(8,128)(2,1)}, bf16[512,960]{0,1:T(8,128)(2,1)}, u32[]{:S(2)}, u32[]{:S(2)}) collective-permute-start(bf16[512,960]{0,1:T(8,128)(2,1)} %bitcast.275), channel_id=1, source_target_pairs={{0,1},{1,0},{2,3},{3,2},{4,5},{5,4},{6,7},{7,6},{8,9},{9,8},{10,11... | collective-permute-start | bytes 2949128 | tf_op jit(solution)/shard_map/ppermute | solution.py:604
  428.1 15.4 %collective-permute-start.15 = (bf16[2,2,32,896]{3,2,1,0:T(8,128)(2,1)S(1)}, bf16[2,2,32,896]{3,2,1,0:T(8,128)(2,1)S(1)}, u32[]{:S(2)}, u32[]{:S(2)}) collective-permute-start(bf16[2,2,32,896]{3,2,1,0:T(8,128)(2,1)S(1)} %dynamic-slice_bitcast_fusion.13), channel_id=1, source_target_pairs={{0,2},{2,0},{4,6},{6,4},{8,10},{10,8},{12,14},{14,12},{16,18},{18,... | collective-permute-start | bytes 688136 | tf_op jit(solution)/shard_map/ppermute | solution.py:608
  431.5 36.0 %collective-permute-start.25 = (bf16[2,2,544,256]{3,2,1,0:T(8,128)(2,1)S(1)}, bf16[2,2,544,256]{3,2,1,0:T(8,128)(2,1)S(1)}, u32[]{:S(2)}, u32[]{:S(2)}) collective-permute-start(bf16[2,2,544,256]{3,2,1,0:T(8,128)(2,1)S(1)} %dynamic-slice_bitcast_fusion.5), channel_id=1, source_target_pairs={{0,2},{2,0},{4,6},{6,4},{8,10},{10,8},{12,14},{14,12},{16,18},{18,... | collective-permute-start | bytes 3342344 | tf_op jit(solution)/shard_map/ppermute | solution.py:608
  438.6 29.2 %collective-permute-start.22 = (bf16[2,2,544,256]{3,2,1,0:T(8,128)(2,1)S(1)}, bf16[2,2,544,256]{3,2,1,0:T(8,128)(2,1)S(1)}, u32[]{:S(2)}, u32[]{:S(2)}) collective-permute-start(bf16[2,2,544,256]{3,2,1,0:T(8,128)(2,1)S(1)} %dynamic-slice_bitcast_fusion.6), channel_id=1, source_target_pairs={{0,4},{2,6},{4,0},{6,2},{8,12},{10,14},{12,8},{14,10},{16,20},{18,... | collective-permute-start | bytes 3342344 | tf_op jit(solution)/shard_map/ppermute | solution.py:608
  443.5 23.9 %collective-permute-start.13 = (bf16[2,2,32,896]{3,2,1,0:T(8,128)(2,1)S(1)}, bf16[2,2,32,896]{3,2,1,0:T(8,128)(2,1)S(1)}, u32[]{:S(2)}, u32[]{:S(2)}) collective-permute-start(bf16[2,2,32,896]{3,2,1,0:T(8,128)(2,1)S(1)} %dynamic-slice_bitcast_fusion.14), channel_id=1, source_target_pairs={{0,4},{2,6},{4,0},{6,2},{8,12},{10,14},{12,8},{14,10},{16,20},{18,... | collective-permute-start | bytes 688136 | tf_op jit(solution)/shard_map/ppermute | solution.py:608
  469.3 64.3 %collective-permute-start.26 = (bf16[2,2,544,256]{3,2,0,1:T(8,128)(2,1)}, bf16[2,2,544,256]{3,2,0,1:T(8,128)(2,1)}, u32[]{:S(2)}, u32[]{:S(2)}) collective-permute-start(bf16[2,2,544,256]{3,2,0,1:T(8,128)(2,1)} %fusion.21), channel_id=1, source_target_pairs={{0,16},{2,18},{4,20},{6,22},{8,24},{10,26},{12,28},{14,30},{16,0},... | collective-permute-start | bytes 3342344 | tf_op jit(solution)/shard_map/ppermute | solution.py:608
  470.0 57.4 %collective-permute-start.16 = (bf16[2,2,32,896]{3,2,1,0:T(8,128)(2,1)}, bf16[2,2,32,896]{3,2,1,0:T(8,128)(2,1)}, u32[]{:S(2)}, u32[]{:S(2)}) collective-permute-start(bf16[2,2,32,896]{3,2,1,0:T(8,128)(2,1)} %fusion.39), channel_id=1, source_target_pairs={{0,16},{2,18},{4,20},{6,22},{8,24},{10,26},{12,28},{14,30},{16,0},... | collective-permute-start | bytes 688136 | tf_op jit(solution)/shard_map/ppermute | solution.py:608
  535.1 14.3 %collective-permute-start.27 = (bf16[2,544,256]{2,1,0:T(8,128)(2,1)S(1)}, bf16[2,544,256]{2,1,0:T(8,128)(2,1)S(1)}, u32[]{:S(2)}, u32[]{:S(2)}) collective-permute-start(bf16[2,544,256]{2,1,0:T(8,128)(2,1)S(1)} %dynamic-slice_bitcast_fusion.12), channel_id=1, source_target_pairs={{0,8},{2,10},{4,12},{6,14},{8,0},{10,2},{12,4},{14,6},{16,24},{18,... | collective-permute-start | bytes 1671176 | tf_op jit(solution)/shard_map/ppermute | solution.py:608
  (41 other events, 299.6 us)
Sparse Core Ops, SparseCore 0:
  11.8 136.8 all-gather.1
